TPU v7x, 768 devices: a whole 4x8x12 slice. The times are simulated.
768 devices in a mesh: grp: 12 (over z), tile: 16 (over y, core), rep: 4 (over x).
Axes of the slice: x: 4, y: 8, z: 12, core: 2. Of those that a mesh axis runs over, the one named last changes fastest.
Arguments:
- amplitudes: bfloat16 [3072, 8, 4096], P(('grp', 'tile')), may hold values from -6 to 6
- tile_blocks: int32 [3072, 2], P(('grp', 'tile')), may hold values from 0 to 127, as said below
- live_rows: int32 [3072], P(('grp', 'tile')), may hold values from 4 to 8
- ladder_factors: bfloat16 [128, 2, 32, 4096], P('tile', None, 'rep'), may hold values from -0.3125 to 0.3125
- cycle_coupling: bfloat16 [64, 8, 8], replicated, may hold values from -2 to 2
- block_owner: int32 [128], replicated, may hold values from 0 to 127, as said below
Outputs:
- residual: bfloat16 [3072, 8, 4096], P(('grp', 'tile'), 'rep')
Inputs may be any that keep to these rules, and one draw needn't show every extreme that they name: Column 0 is an occupied-pair block below 64, column 1 a virtual-pair block below 128. Among the tiles of one index pair of grp and tile, at most 2 have blocks whose owner position block_owner[tile_blocks[k, 1]] // 8 is the same; in every group of grp some owner has exactly 2 from every index of tile. `block_owner`: A permutation of the virtual-pair blocks.
All inputs are finite; a program needn't handle non-finite values.
Results may differ from a plain program's by a relative error of at most 0.0036.
Values may be sent and summed in bfloat16 or wider, within the bound.
No kernel may reach another device: no remote copies, remote signals or barrier semaphores. Data moves between devices by JAX's collectives and lax.ppermute only.
A program may use at most 64 MiB of HBM per device.

v0:
```python
import jax
import jax.numpy as jnp
from jax import lax
from jax.sharding import PartitionSpec as P

VB = 64
CAP = 2


def aux_group(total, load):
    group = max(1, 512 // max(load, 1))
    group = min(group, total)
    for trial in range(group, 0, -1):
        return trial
    return 1


def ladder_block(buffer, labels, factors):
    count = buffer.shape[0]
    rows = buffer.shape[1]
    depth = factors.shape[2]
    index = labels.astype(jnp.int32)
    grid = buffer.reshape(count, rows, VB, VB)
    group = aux_group(depth, count * rows)

    def step(total, start):
        portion = lax.dynamic_slice_in_dim(factors, start * group, group, 2)
        picked = jnp.take(portion, index, axis=0).reshape(count, 2, group, VB, VB)
        middle = jnp.einsum(
            "kqac,kpcd->kpqad", picked[:, 0], grid, preferred_element_type=jnp.float32
        ).astype(jnp.bfloat16)
        total = total + jnp.einsum(
            "kpqad,kqbd->kpab", middle, picked[:, 1], preferred_element_type=jnp.float32
        )
        return (total, None)

    start_total = jnp.zeros((count, rows, VB, VB), jnp.float32)
    total, unused = lax.scan(step, start_total, jnp.arange(depth // group))
    return total.reshape(count, rows, VB * VB)


def send_back(values):
    return lax.all_to_all(values, "tile", split_axis=0, concat_axis=0, tiled=True)


def rep_total(values):
    return lax.psum_scatter(values, "rep", scatter_dimension=1, tiled=True)


def local(amplitudes, tile_blocks, live_rows, ladder_factors, cycle_coupling, block_owner):
    rows = amplitudes.shape[1]
    cells = amplitudes.shape[2]
    peers = lax.axis_size("tile")
    reps = lax.axis_size("rep")
    owned = ladder_factors.shape[0]
    capacity = CAP
    share = rows // reps
    lead = lax.axis_index("rep") * share
    live = jnp.arange(rows)[None, :] < live_rows[:, None]
    masked = jnp.where(live[:, :, None], amplitudes, jnp.zeros_like(amplitudes))
    pick = tile_blocks[:, 1:2] == jnp.arange(block_owner.shape[0])[None, :]
    place = jnp.sum(jnp.where(pick, block_owner[None, :], 0), axis=1)
    target = place // owned
    within = place % owned
    onehot_target = (target[:, None] == jnp.arange(peers)[None, :]).astype(jnp.int32)
    earlier = jnp.cumsum(onehot_target, axis=0) - onehot_target
    rank_own = jnp.sum(earlier * onehot_target, axis=1)
    slot = target * capacity + rank_own
    slots_total = peers * capacity
    spread = (slot[None, :] == jnp.arange(slots_total)[:, None]).astype(jnp.bfloat16)
    chosen = (tile_blocks[:, 0:1] == jnp.arange(cycle_coupling.shape[0])[None, :]).astype(
        jnp.bfloat16
    )
    coupling = jnp.einsum(
        "kn,npq->kpq", chosen, cycle_coupling, preferred_element_type=jnp.float32
    ).astype(jnp.bfloat16)
    coupling_rows = lax.dynamic_slice_in_dim(coupling, lead, share, 1)
    cycle = jnp.einsum("kpq,kqx->kpx", coupling_rows, masked, preferred_element_type=jnp.float32)
    width = masked.shape[1]
    packed = jnp.einsum("sk,krx->srx", spread, masked, preferred_element_type=jnp.float32).astype(
        jnp.bfloat16
    )
    packed = packed.reshape(peers, capacity, width, cells)
    labels = jnp.sum(spread.astype(jnp.float32) * within[None, :].astype(jnp.float32), axis=1)
    labels = labels.astype(jnp.bfloat16).reshape(peers, capacity)
    buffer = lax.all_to_all(packed, "tile", split_axis=0, concat_axis=0, tiled=True)
    tags = lax.all_to_all(labels, "tile", split_axis=0, concat_axis=0, tiled=True)
    sources = buffer.shape[0]
    slots = buffer.shape[1]
    terms = ladder_block(
        buffer.reshape(sources * slots, width, cells), tags.reshape(sources * slots), ladder_factors
    )
    partial_value = terms.reshape(sources, slots, width, cells)
    returned = send_back(partial_value)
    mine = jnp.take(returned.reshape(slots_total, width, cells), slot, axis=0)
    ladder_rows = rep_total(mine)
    return (ladder_rows + cycle).astype(jnp.bfloat16)


def solution(mesh):
    placed = (
        P(("grp", "tile"), None, None),
        P(("grp", "tile"), None),
        P(("grp", "tile")),
        P("tile", None, "rep", None),
        P(),
        P(),
    )
    return jax.shard_map(
        local,
        mesh=mesh,
        in_specs=placed,
        out_specs=P(("grp", "tile"), "rep", None),
        check_vma=False,
    )
```

profile of v0, /device:TPU:1, one launch (start us, length us, event | category | flops | bytes accessed | tf_op | source)
XLA Modules:
  0.0 337.8 jit_solution(11743313331406471465)
XLA Ops:
  6.5 0.8 slice_bitcast_fusion.6
  7.3 0.8 select_reduce_fusion.1
  8.5 0.7 convert_element_type.67
  9.3 13.8 %all-to-all-start = ((bf16[16,1,2]{2,1,0:T(2,128)(2,1)}), bf16[16,1,2]{2,1,0:T(2,128)(2,1)S(1)}, u32[]{:S(2)}, u32[]{:S(2)}) async-start(bf16[16,1,2]{2,1,0:T(2,128)(2,1)} %convert_element_type.67), calls=%async_computation | async-start | bytes 16384 | tf_op jit(solution)/shard_map/all_to_all | solution.py:87
  23.0 0.7 iota_compare_fusion.1
  23.8 1.4 broadcast_select_fusion.2
  25.1 1.4 convolution_convert_fusion
  26.5 2.7 reshape.183
  29.2 5.7 %copy.30 = bf16[16,2,8,4096]{3,1,2,0:T(2,128)(2,1)} copy(bf16[16,2,8,4096]{3,1,0,2:T(2,128)(2,1)} %reshape.183) | data formatting | bytes 4194304 | tf_op jit(solution)/shard_map/reshape | solution.py:83
  34.9 7.3 %all-to-all-start.1 = ((bf16[16,2,8,4096]{3,1,2,0:T(2,128)(2,1)}), bf16[16,2,8,4096]{3,1,2,0:T(2,128)(2,1)}, u32[]{:S(2)}, u32[]{:S(2)}) async-start(bf16[16,2,8,4096]{3,1,2,0:T(2,128)(2,1)} %copy.30), calls=%async_computation.1 | async-start | bytes 4194304 | tf_op jit(solution)/shard_map/all_to_all | solution.py:86
  42.3 48.9 %all-to-all-done.1 = bf16[16,2,8,4096]{3,1,2,0:T(2,128)(2,1)} async-done(((bf16[16,2,8,4096]{3,1,2,0:T(2,128)(2,1)}), bf16[16,2,8,4096]{3,1,2,0:T(2,128)(2,1)}, u32[]{:S(2)}, u32[]{:S(2)}) %all-to-all-start.1) | async-done | bytes 2097184 | tf_op jit(solution)/shard_map/all_to_all | solution.py:86
  91.3 2.9 copy.31
  94.2 5.5 %reshape_reshape.6 = bf16[32,8,64,64]{3,2,1,0:T(8,128)(2,1)} reshape(bf16[16,2,8,4096]{3,2,1,0:T(8,128)(2,1)S(1)} %copy.31) | data formatting | bytes 4194304 | tf_op jit(solution)/shard_map/reshape;reshape | solution.py:23
  99.7 79.5 %while.11 = (s32[]{:T(128)}, f32[32,8,64,64]{3,2,1,0:T(8,128)}, s32[32]{0:T(128)S(1)}, s32[4]{0:T(128)S(1)}, bf16[8,2,8,4096]{3,2,1,0:T(8,128)(2,1)}, /*index=5*...) while((s32[]{:T(128)}, f32[32,8,64,64]{3,2,1,0:T(8,128)}, ...), condition=%wide.region_5.6_spmd.clone, body=%wide.region_4.5_spmd.clone.sunk | while | flops 541590848 | bytes 20452204 | solution.py:38
  99.7 0.6 dynamic_slice.19
  100.9 1.5 constant_dynamic-slice_fusion.2
  102.5 2.7 gather_fusion
  105.2 1.0 copy.43
  106.2 2.3 gather.20
  108.5 1.8 broadcast_select_fusion.4
  110.4 8.3 %bitcast_add_fusion.3 = f32[32,8,64,64]{3,2,1,0:T(8,128)} fusion(f32[32,8,64,64]{3,2,1,0:T(8,128)} %get-tuple-element.125, pred[]{:T(512)S(6)} %compare.30, bf16[32,8,64,64]{3,2,1,0:T(8,128)(2,1)} %get-tuple-element.139, bf16[32,2,2,64,64]{4,3,2,0,1:T(8,128)(2,1)S(1)} %broadcast_select_fusion.4), kind=kOutput, calls=%fused_computation.2.clone.1 | convolution fusion | flops 541065216 | bytes 11534337 | tf_op jit(solution)/shard_map/while/body/eval_jaxpr/kpqad,kqbd->kpab/dot_general | solution.py:32
  118.6 0.6 dynamic_slice.19
  119.9 1.5 constant_dynamic-slice_fusion.2
  121.4 2.7 gather_fusion
  124.1 1.0 copy.43
  125.1 2.3 gather.20
  127.5 1.8 broadcast_select_fusion.4
  129.3 9.5 %bitcast_add_fusion.3 = f32[32,8,64,64]{3,2,1,0:T(8,128)} fusion(f32[32,8,64,64]{3,2,1,0:T(8,128)} %get-tuple-element.125, pred[]{:T(512)S(6)} %compare.30, bf16[32,8,64,64]{3,2,1,0:T(8,128)(2,1)} %get-tuple-element.139, bf16[32,2,2,64,64]{4,3,2,0,1:T(8,128)(2,1)S(1)} %broadcast_select_fusion.4), kind=kOutput, calls=%fused_computation.2.clone.1 | convolution fusion | flops 541065216 | bytes 11534337 | tf_op jit(solution)/shard_map/while/body/eval_jaxpr/kpqad,kqbd->kpab/dot_general | solution.py:32
  138.8 0.6 dynamic_slice.19
  140.1 1.5 constant_dynamic-slice_fusion.2
  141.6 2.7 gather_fusion
  144.3 1.0 copy.43
  145.3 2.3 gather.20
  147.7 1.8 broadcast_select_fusion.4
  149.5 9.5 %bitcast_add_fusion.3 = f32[32,8,64,64]{3,2,1,0:T(8,128)} fusion(f32[32,8,64,64]{3,2,1,0:T(8,128)} %get-tuple-element.125, pred[]{:T(512)S(6)} %compare.30, bf16[32,8,64,64]{3,2,1,0:T(8,128)(2,1)} %get-tuple-element.139, bf16[32,2,2,64,64]{4,3,2,0,1:T(8,128)(2,1)S(1)} %broadcast_select_fusion.4), kind=kOutput, calls=%fused_computation.2.clone.1 | convolution fusion | flops 541065216 | bytes 11534337 | tf_op jit(solution)/shard_map/while/body/eval_jaxpr/kpqad,kqbd->kpab/dot_general | solution.py:32
  160.3 1.5 constant_dynamic-slice_fusion.2
  161.8 2.7 gather_fusion
  164.5 1.0 copy.43
  165.5 2.3 gather.20
  167.9 1.8 broadcast_select_fusion.4
  169.7 9.5 %bitcast_add_fusion.3 = f32[32,8,64,64]{3,2,1,0:T(8,128)} fusion(f32[32,8,64,64]{3,2,1,0:T(8,128)} %get-tuple-element.125, pred[]{:T(512)S(6)} %compare.30, bf16[32,8,64,64]{3,2,1,0:T(8,128)(2,1)} %get-tuple-element.139, bf16[32,2,2,64,64]{4,3,2,0,1:T(8,128)(2,1)S(1)} %broadcast_select_fusion.4), kind=kOutput, calls=%fused_computation.2.clone.1 | convolution fusion | flops 541065216 | bytes 11534337 | tf_op jit(solution)/shard_map/while/body/eval_jaxpr/kpqad,kqbd->kpab/dot_general | solution.py:32
  179.2 7.9 %reshape_reshape.7 = f32[16,2,8,4096]{3,2,1,0:T(8,128)} reshape(f32[32,8,64,64]{3,2,1,0:T(8,128)} %get-tuple-element.37) | data formatting | bytes 8388608 | tf_op jit(solution)/shard_map/reshape;reshape | solution.py:93
  187.1 5.0 %all-to-all-start.2 = ((f32[16,2,8,4096]{3,2,1,0:T(8,128)}), f32[16,2,8,4096]{3,2,1,0:T(8,128)}, u32[]{:S(2)}, u32[]{:S(2)}) async-start(f32[16,2,8,4096]{3,2,1,0:T(8,128)} %reshape_reshape.7), calls=%async_computation.2 | async-start | bytes 8388608 | tf_op jit(solution)/shard_map/all_to_all | solution.py:43
  192.2 93.5 %all-to-all-done.2 = f32[16,2,8,4096]{3,2,1,0:T(8,128)} async-done(((f32[16,2,8,4096]{3,2,1,0:T(8,128)}), f32[16,2,8,4096]{3,2,1,0:T(8,128)}, u32[]{:S(2)}, u32[]{:S(2)}) %all-to-all-start.2) | async-done | bytes 4194336 | tf_op jit(solution)/shard_map/all_to_all | solution.py:43
  285.7 2.9 gather_fusion.1
  288.8 2.6 copy.32
  291.7 36.9 %reduce-scatter.2.cloned.1.call-done = f32[16,2,4096]{2,0,1:T(8,128)} async-done(((f32[16,8,4096]{2,0,1:T(8,128)}), f32[16,2,4096]{2,0,1:T(8,128)}) %reduce-scatter.2.cloned.1.call-update) | async-done | bytes 524304 | tf_op jit(solution)/shard_map/reduce_scatter | solution.py:47
  328.6 2.3 fusion.12
  (34 shorter events, 1.8 us)
Async XLA Ops:
  6.5 284.9 %copy-start = (bf16[64,8,8]{0,2,1:T(8,128)(2,1)S(1)}, bf16[64,8,8]{0,2,1:T(8,128)(2,1)}, u32[]{:S(2)}) copy-start(bf16[64,8,8]{0,2,1:T(8,128)(2,1)} %param.12) | copy-start | bytes 24580
  9.3 25.7 %all-to-all-start = ((bf16[16,1,2]{2,1,0:T(2,128)(2,1)}), bf16[16,1,2]{2,1,0:T(2,128)(2,1)S(1)}, u32[]{:S(2)}, u32[]{:S(2)}) async-start(bf16[16,1,2]{2,1,0:T(2,128)(2,1)} %convert_element_type.67), calls=%async_computation | async-start | bytes 16384 | tf_op jit(solution)/shard_map/all_to_all | solution.py:87
  34.9 56.3 %all-to-all-start.1 = ((bf16[16,2,8,4096]{3,1,2,0:T(2,128)(2,1)}), bf16[16,2,8,4096]{3,1,2,0:T(2,128)(2,1)}, u32[]{:S(2)}, u32[]{:S(2)}) async-start(bf16[16,2,8,4096]{3,1,2,0:T(2,128)(2,1)} %copy.30), calls=%async_computation.1 | async-start | bytes 4194304 | tf_op jit(solution)/shard_map/all_to_all | solution.py:86
  187.1 98.6 %all-to-all-start.2 = ((f32[16,2,8,4096]{3,2,1,0:T(8,128)}), f32[16,2,8,4096]{3,2,1,0:T(8,128)}, u32[]{:S(2)}, u32[]{:S(2)}) async-start(f32[16,2,8,4096]{3,2,1,0:T(8,128)} %reshape_reshape.7), calls=%async_computation.2 | async-start | bytes 8388608 | tf_op jit(solution)/shard_map/all_to_all | solution.py:43
  192.1 136.6 %reduce-scatter.2.cloned.1.call-start = ((), (), s32[]{:S(2)}) async-start(), calls=%async_computation.4 | async-start | bytes 2621440 | tf_op jit(solution)/shard_map/reduce_scatter | solution.py:47
Sparse Core Ops, SparseCore 0:
  291.5 37.0 reduce-scatter.1
where the time goes:
time: 339 us; the launch traced here: 338 us
  waiting for transfers between devices  179 us (53%)
  local copies, waits for them, and re-layouts  64.5 us (19%)
  matrix products  40.6 us (12%)
  starting transfers between devices  26.1 us (8%)
  between operations  13.5 us (4%)
  other arithmetic  11.1 us (3%)
    all_to_all x1, waiting for transfers between devices, send_back(): lax.all_to_all(values, 'tile', split_axis=0, concat_axis=0, tiled=True)  93.5 us
    all_to_all x1, waiting for transfers between devices, local(): lax.all_to_all(packed, 'tile', split_axis=0, concat_axis=0, tiled=True)  48.9 us
    reduce_scatter x1, waiting for transfers between devices, rep_total(): return lax.psum_scatter(values, 'rep', scatter_dimension=1, tiled=True)  36.9 us
    dot_general x4, matrix products, step(): jnp.einsum('kpqad,kqbd->kpab', middle, picked[:, 1], preferred_element_ty...  36.7 us
    gather x12, local copies, waits for them, and re-layouts, step(): picked = jnp.take(portion, index, axis=0).reshape(count, 2, group, VB, VB)  24.1 us
    all_to_all x1, starting transfers between devices, local(): lax.all_to_all(labels, 'tile', split_axis=0, concat_axis=0, tiled=True)  13.8 us
    reshape x2, local copies, waits for them, and re-layouts, local(): packed = packed.reshape(peers, capacity, width, cells)  8.4 us
    another operation x1, local copies, waits for them, and re-layouts, local(): partial_value = terms.reshape(sources, slots, width, cells)  7.89 us
  transfers between devices with their start and end apart: 4, of which 3 were waited for; matrix products, arithmetic and copies ran while one was open for 4% of the time, Pallas kernels for 0%

commit v1 on v0

v1 whole, which is shorter than its diff:
```python
import jax
import jax.numpy as jnp
from jax import lax
from jax.experimental import pallas as pl
from jax.experimental.pallas import tpu as pltpu
from jax.sharding import PartitionSpec as P

VB = 64
CAP = 2
GROUP = 4
LANES = 128
LABEL_ROWS = 16
UNROLL = 8
SMALL_VMEM = 16 * 1024 * 1024
LADDER_VMEM = 40 * 1024 * 1024


def low_lanes(shape):
    return lax.broadcasted_iota(jnp.int32, shape, 1) < VB


def join(first, second):
    low = low_lanes(first.shape)
    return (
        jnp.where(low, first, pltpu.roll(second, VB, 1)),
        jnp.where(low, pltpu.roll(first, VB, 1), second),
    )


def spread_rows(block, scratch):
    for t in range(block.shape[1] // LANES):
        scratch[t * 8 : (t + 1) * 8, :] = block[:, t * LANES : (t + 1) * LANES]


def factor_kernel(factor_ref, out_ref, scratch, woven):
    def one(v, carry):
        for side in range(2):
            spread_rows(factor_ref[v, side].astype(jnp.float32), scratch.at[side])
            for half in range(2):
                rows = [
                    scratch[side, pl.ds(half * GROUP + q, 32, stride=8), :] for q in range(GROUP)
                ]
                for pair in range(GROUP // 2):
                    even, odd = join(rows[2 * pair], rows[2 * pair + 1])
                    lanes = slice(pair * LANES, (pair + 1) * LANES)
                    if side == 0:
                        out_ref[half, v, 0, 0:32, lanes] = even.astype(jnp.bfloat16)
                        out_ref[half, v, 0, 32:64, lanes] = odd.astype(jnp.bfloat16)
                    else:
                        spot = half * 2 + pair
                        woven[spot, pl.ds(0, 32, stride=2), :] = even
                        woven[spot, pl.ds(1, 32, stride=2), :] = odd
                        out_ref[half, v, 1, :, lanes] = woven[spot].astype(jnp.bfloat16)
        return carry

    lax.fori_loop(0, factor_ref.shape[0], one, 0)


def arrange_factors(factors):
    owned = factors.shape[0]
    return pl.pallas_call(
        factor_kernel,
        out_shape=jax.ShapeDtypeStruct((2, owned, 2, VB, GROUP * VB), jnp.bfloat16),
        in_specs=[pl.BlockSpec(memory_space=pltpu.VMEM)],
        out_specs=pl.BlockSpec(memory_space=pltpu.VMEM),
        scratch_shapes=[
            pltpu.VMEM((2, 256, LANES), jnp.float32),
            pltpu.VMEM((4, VB, LANES), jnp.float32),
        ],
        compiler_params=pltpu.CompilerParams(vmem_limit_bytes=SMALL_VMEM),
        name="arrange_factors",
    )(factors)


def pack_kernel(
    lead_ref, blocks_ref, live_ref, owner_ref, amp_ref, out_ref, slot_ref, counts, labels, scratch, woven
):
    peers = out_ref.shape[0]
    owned = owner_ref.shape[0] // peers
    for s in range(peers):
        counts[s] = 0
        for r in range(CAP):
            labels[s, r] = 0
    out_ref[...] = jnp.zeros(out_ref.shape, out_ref.dtype)
    lead = lead_ref[0]
    for k in range(amp_ref.shape[0]):
        place = owner_ref[blocks_ref[1, k]]
        target = place // owned
        rank = counts[target]
        counts[target] = rank + 1
        labels[target, rank] = place - target * owned
        slot_ref[k] = target * CAP + rank
        spot = k % 2
        spread_rows(amp_ref[k].astype(jnp.float32), scratch.at[spot])
        live = live_ref[k]
        rows = [
            jnp.where(lead + p < live, scratch[spot, pl.ds(lead + p, 32, stride=8), :], 0.0)
            for p in range(2)
        ]
        even, odd = join(rows[0], rows[1])
        woven[spot, pl.ds(0, 32, stride=2), :] = even
        woven[spot, pl.ds(1, 32, stride=2), :] = odd
        out_ref[target, pl.ds(pl.multiple_of(rank * VB, VB), VB), :] = woven[spot].astype(jnp.bfloat16)
    row = lax.broadcasted_iota(jnp.int32, (LABEL_ROWS, LANES), 0)
    for s in range(peers):
        tag = jnp.where(row == 0, labels[s, 0], labels[s, 1])
        out_ref[s, CAP * VB :, :] = tag.astype(jnp.float32).astype(jnp.bfloat16)


def pack(lead, tile_blocks, live_rows, block_owner, amplitudes, peers):
    tiles = amplitudes.shape[0]
    smem = pl.BlockSpec(memory_space=pltpu.SMEM)
    vmem = pl.BlockSpec(memory_space=pltpu.VMEM)
    return pl.pallas_call(
        pack_kernel,
        out_shape=(
            jax.ShapeDtypeStruct((peers, CAP * VB + LABEL_ROWS, LANES), jnp.bfloat16),
            jax.ShapeDtypeStruct((tiles,), jnp.int32),
        ),
        in_specs=[smem, smem, smem, smem, vmem],
        out_specs=(vmem, smem),
        scratch_shapes=[
            pltpu.SMEM((peers,), jnp.int32),
            pltpu.SMEM((peers, CAP), jnp.int32),
            pltpu.VMEM((2, 256, LANES), jnp.float32),
            pltpu.VMEM((2, VB, LANES), jnp.float32),
        ],
        compiler_params=pltpu.CompilerParams(vmem_limit_bytes=SMALL_VMEM),
        name="pack_tiles",
    )(lead, tile_blocks, live_rows, block_owner, amplitudes)


def read_labels(buffer_ref, label_vmem, label_smem, sem):
    lane = lax.broadcasted_iota(jnp.int32, (LABEL_ROWS, LANES), 1)
    table = jnp.zeros((LABEL_ROWS, LANES), jnp.float32)
    for s in range(buffer_ref.shape[0]):
        table = jnp.where(lane == s, buffer_ref[s, CAP * VB :, :].astype(jnp.float32), table)
    label_vmem[...] = table.astype(jnp.int32)
    copy = pltpu.make_async_copy(label_vmem, label_smem, sem)
    copy.start()
    copy.wait()


def slot_terms(i, label_smem, buffer, halves):
    peer, rank = i // CAP, i % CAP
    v = label_smem[rank, peer]
    tile = buffer[peer, pl.ds(pl.multiple_of(rank * VB, VB), VB), :].astype(jnp.float32)
    turned = pltpu.roll(tile, VB, 1)
    low = low_lanes(tile.shape)
    upper = [jnp.where(low, rows, 0.0).astype(jnp.bfloat16) for rows in (tile, turned)]
    lower = [jnp.where(low, 0.0, rows).astype(jnp.bfloat16) for rows in (turned, tile)]
    pairs = jnp.concatenate([jnp.concatenate(upper, axis=1), jnp.concatenate(lower, axis=1)], axis=0)
    total = None
    for h in range(halves.shape[0]):
        left = halves[h, v, 0]
        left = jnp.concatenate([left[:, :LANES], left[:, LANES:]], axis=0)
        middle = jnp.dot(left, pairs, preferred_element_type=jnp.float32).astype(jnp.bfloat16)
        rows = [
            jnp.concatenate(
                [middle[:VB, p * LANES : (p + 1) * LANES], middle[VB:, p * LANES : (p + 1) * LANES]],
                axis=1,
            )
            for p in range(2)
        ]
        term = lax.dot_general(
            jnp.concatenate(rows, axis=0),
            halves[h, v, 1],
            (((1,), (1,)), ((), ())),
            preferred_element_type=jnp.float32,
        )
        total = term if total is None else total + term
    flat = [
        jnp.concatenate([total[p * VB : p * VB + 32], total[p * VB + 32 : (p + 1) * VB]], axis=1)
        for p in range(2)
    ]
    return jnp.concatenate(flat, axis=0)


def ladder_kernel(n, more, *refs):
    buffer_ref, half_refs = refs[0], refs[1 : 1 + n]
    earlier_ref = refs[1 + n] if more else None
    out_ref, buffer, halves, label_vmem, label_smem, sems, label_sem = refs[1 + n + more :]
    arrive = pltpu.make_async_copy(buffer_ref, buffer, sems.at[n])
    arrive.start()
    each = halves.shape[0] // n
    copies = [
        pltpu.make_async_copy(half_refs[h], halves.at[pl.ds(h * each, each)], sems.at[h]) for h in range(n)
    ]
    for copy in copies:
        copy.start()
    arrive.wait()
    read_labels(buffer, label_vmem, label_smem, label_sem)
    for copy in copies:
        copy.wait()

    def some(j, carry):
        for k in range(UNROLL):
            i = j * UNROLL + k
            terms = slot_terms(i, label_smem, buffer, halves)
            if more:
                terms = terms + earlier_ref[i]
            out_ref[i] = terms.astype(out_ref.dtype)
        return carry

    lax.fori_loop(0, out_ref.shape[0] // UNROLL, some, 0)


def ladder_terms(buffer, halves, earlier=None):
    peers = buffer.shape[0]
    slots = peers * CAP
    n, more = len(halves), int(earlier is not None)
    vmem, anywhere = pl.BlockSpec(memory_space=pltpu.VMEM), pl.BlockSpec(memory_space=pl.ANY)
    passes = slots * n * 2 * 2 * 2 * VB * VB * LANES
    return pl.pallas_call(
        lambda *refs: ladder_kernel(n, more, *refs),
        out_shape=jax.ShapeDtypeStruct((slots, VB, LANES), jnp.bfloat16 if more else jnp.float32),
        in_specs=[anywhere] * (1 + n) + [vmem] * more,
        out_specs=vmem,
        scratch_shapes=[
            pltpu.VMEM(buffer.shape, buffer.dtype),
            pltpu.VMEM((n * halves[0].shape[0],) + halves[0].shape[1:], halves[0].dtype),
            pltpu.VMEM((LABEL_ROWS, LANES), jnp.int32),
            pltpu.SMEM((LABEL_ROWS, LANES), jnp.int32),
            pltpu.SemaphoreType.DMA((n + 1,)),
            pltpu.SemaphoreType.DMA,
        ],
        compiler_params=pltpu.CompilerParams(vmem_limit_bytes=LADDER_VMEM),
        cost_estimate=pl.CostEstimate(flops=passes // 100, bytes_accessed=n << 19, transcendentals=0),
        name="ladder_terms",
    )(buffer, *halves, *([earlier] if more else []))


def finish_kernel(slot_ref, returned_ref, cycle_ref, out_ref, scratch):
    for k in range(out_ref.shape[0]):
        spot = k % 2
        block = returned_ref[slot_ref[k]].astype(jnp.float32)
        for p in range(2):
            scratch[spot, pl.ds(p, 32, stride=2), :] = block[p * 32 : (p + 1) * 32]
        for t in range(32):
            lanes = slice(t * LANES, (t + 1) * LANES)
            total = scratch[spot, 2 * t : 2 * t + 2, :] + cycle_ref[k, :, lanes]
            out_ref[k, :, lanes] = total.astype(jnp.bfloat16)


def finish(slot, returned, cycle):
    vmem = pl.BlockSpec(memory_space=pltpu.VMEM)
    return pl.pallas_call(
        finish_kernel,
        out_shape=jax.ShapeDtypeStruct(cycle.shape, jnp.bfloat16),
        in_specs=[pl.BlockSpec(memory_space=pltpu.SMEM), vmem, vmem],
        out_specs=vmem,
        scratch_shapes=[pltpu.VMEM((2, VB, LANES), jnp.float32)],
        compiler_params=pltpu.CompilerParams(vmem_limit_bytes=SMALL_VMEM),
        name="finish_tiles",
    )(slot, returned, cycle)


def cycle_terms(lead, share, amplitudes, tile_blocks, live_rows, cycle_coupling):
    tiles, rows, cells = amplitudes.shape
    chosen = (tile_blocks[:, 0:1] == jnp.arange(cycle_coupling.shape[0])[None, :]).astype(jnp.bfloat16)
    mine = lax.dynamic_slice_in_dim(cycle_coupling, lead, share, 1)
    coupling = jnp.einsum("kn,npq->kpq", chosen, mine, preferred_element_type=jnp.float32)
    live = jnp.arange(rows)[None, :] < live_rows[:, None]
    same = jnp.eye(tiles, dtype=bool)
    mixing = jnp.where(
        same[:, None, :, None] & live[:, None, None, :], coupling[:, :, None, :], 0.0
    ).astype(jnp.bfloat16)
    cycle = jnp.dot(
        mixing.reshape(tiles * share, tiles * rows),
        amplitudes.reshape(tiles * rows, cells),
        preferred_element_type=jnp.float32,
    )
    return cycle.reshape(tiles, share, cells)


def local(amplitudes, tile_blocks, live_rows, ladder_factors, cycle_coupling, block_owner):
    peers = lax.axis_size("tile")
    reps = lax.axis_size("rep")
    share = amplitudes.shape[1] // reps
    lead = lax.axis_index("rep") * share
    up = [(i, (i + 1) % reps) for i in range(reps)]
    down = [(i, (i - 1) % reps) for i in range(reps)]

    own = arrange_factors(ladder_factors)
    below = lax.ppermute(own, "rep", up)
    above = lax.ppermute(own, "rep", down)
    far_first = lax.ppermute(below[0:1], "rep", up)
    far_second = lax.ppermute(above[1:2], "rep", down)

    packed, slot = pack(
        lead.astype(jnp.int32).reshape(1), tile_blocks.T, live_rows, block_owner, amplitudes, peers
    )
    buffer = lax.all_to_all(packed, "tile", split_axis=0, concat_axis=0, tiled=True)
    cycle = cycle_terms(lead, share, amplitudes, tile_blocks, live_rows, cycle_coupling)
    earlier = ladder_terms(buffer, (own, below, above))
    terms = ladder_terms(buffer, (far_first, far_second), earlier)
    returned = lax.all_to_all(terms, "tile", split_axis=0, concat_axis=0, tiled=True)
    return finish(slot, returned, cycle)


def solution(mesh):
    placed = (
        P(("grp", "tile"), None, None),
        P(("grp", "tile"), None),
        P(("grp", "tile")),
        P("tile", None, "rep", None),
        P(),
        P(),
    )
    return jax.shard_map(
        local,
        mesh=mesh,
        in_specs=placed,
        out_specs=P(("grp", "tile"), "rep", None),
        check_vma=False,
    )
```

time: 339 us -> 85 us (0.25)
  waiting for transfers between devices: 179 us -> 23.3 us
  local copies, waits for them, and re-layouts: 64.5 us -> 6.28 us
  matrix products: 40.6 us -> 0.98 us
  Pallas kernels: 0 us -> 20.6 us
  between operations: 13.5 us -> 0.2 us
  other arithmetic: 11.1 us -> 0.1 us
  starting transfers between devices: 26.1 us -> 32.9 us
    all_to_all x2 -> x1, waiting for transfers between devices: 93.5 us -> 15.7 us  [local(): lax.all_to_all(terms, 'tile', split_axis=0, concat_axis=0, tiled=True)]
    all_to_all x1, waiting for transfers between devices: 48.9 us -> 7.58 us  [local(): lax.all_to_all(packed, 'tile', split_axis=0, concat_axis=0, tiled=True)]
    dot_general x6 -> x1, matrix products: 40.5 us -> 0.79 us  [cycle_terms(): jnp.dot(mixing.reshape(tiles * share, tiles * rows), amplitudes.reshape(t...]
    reduce_scatter x1 -> x0, waiting for transfers between devices: 36.9 us -> none  [rep_total(): return lax.psum_scatter(values, 'rep', scatter_dimension=1, tiled=True)]
    gather x13 -> x0, local copies, waits for them, and re-layouts: 27 us -> none  [the longest x12 24.1 us: step(): picked = jnp.take(portion, index, axis=0).reshape(count, 2, group, VB, VB)]
    pallas_call x0 -> x5, Pallas kernels: none -> 20.6 us  [the longest x2 15.8 us: ladder_terms(): pl.pallas_call(lambda *refs: ladder_kernel(n, more, *refs), out_shape=jax...]
    ppermute x0 -> x4, starting transfers between devices: none -> 15.4 us  [the longest x1 4.27 us: local(): far_second = lax.ppermute(above[1:2], 'rep', down)]
    all_to_all x2 -> x1, starting transfers between devices: 18.7 us -> 3.61 us  [local(): lax.all_to_all(terms, 'tile', split_axis=0, concat_axis=0, tiled=True)]
  transfers between devices with their start and end apart: 4 -> 6, of which waited for: 3 -> 2; matrix products, arithmetic and copies ran while one was open for 4% -> 5% of each run, Pallas kernels for 0% -> 14%
where the time goes in v1:
time: 85 us; the launch traced here: 84.2 us
  starting transfers between devices  32.9 us (39%)
  waiting for transfers between devices  23.3 us (27%)
  Pallas kernels  20.6 us (24%)
  local copies, waits for them, and re-layouts  6.28 us (7%)
  matrix products  0.98 us (1%)
    pallas_call x2, Pallas kernels, ladder_terms(): pl.pallas_call(lambda *refs: ladder_kernel(n, more, *refs), out_shape=jax...  15.8 us
    all_to_all x1, waiting for transfers between devices, local(): lax.all_to_all(terms, 'tile', split_axis=0, concat_axis=0, tiled=True)  15.7 us
    all_to_all x1, starting transfers between devices, local(): lax.all_to_all(packed, 'tile', split_axis=0, concat_axis=0, tiled=True)  13.8 us
    all_to_all x1, waiting for transfers between devices, local(): lax.all_to_all(packed, 'tile', split_axis=0, concat_axis=0, tiled=True)  7.58 us
    ppermute x1, starting transfers between devices, local(): far_second = lax.ppermute(above[1:2], 'rep', down)  4.27 us
    ppermute x1, starting transfers between devices, local(): far_first = lax.ppermute(below[0:1], 'rep', up)  4.03 us
    ppermute x1, starting transfers between devices, local(): below = lax.ppermute(own, 'rep', up)  3.95 us
    all_to_all x1, starting transfers between devices, local(): lax.all_to_all(terms, 'tile', split_axis=0, concat_axis=0, tiled=True)  3.61 us
  transfers between devices with their start and end apart: 6, of which 2 were waited for; matrix products, arithmetic and copies ran while one was open for 5% of the time, Pallas kernels for 14%

profile of v1, /device:TPU:1, one launch (start us, length us, event | category | flops | bytes accessed | tf_op | source)
XLA Modules:
  0.0 84.2 jit_solution(14451606289430542004)
XLA Ops:
  0.0 0.0 copy-start
  0.0 0.0 copy-start.1
  0.0 1.2 %copy-done.1 = bf16[8,2,8,4096]{3,2,1,0:T(8,128)(2,1)S(1)} copy-done((bf16[8,2,8,4096]{3,2,1,0:T(8,128)(2,1)S(1)}, bf16[8,2,8,4096]{3,2,1,0:T(8,128)(2,1)}, u32[]{:S(2)}) %copy-start.1) | copy-done | bytes 1048600
  1.2 0.0 copy-start.6
  1.2 1.2 %arrange_factors.1.refs_1_ = bf16[2,8,2,64,256]{4,3,2,1,0:T(8,128)(2,1)S(1)} custom-call(bf16[8,2,8,4096]{3,2,1,0:T(8,128)(2,1)S(1)} %copy-done.1), custom_call_target="tpu_custom_call" | custom-call | tf_op jit(solution)/shard_map/arrange_factors/pallas_call | solution.py:61
  2.5 3.9 %collective-permute-start = (bf16[2,8,2,64,256]{4,3,2,1,0:T(8,128)(2,1)S(1)}, bf16[2,8,2,64,256]{4,3,2,1,0:T(8,128)(2,1)S(1)}, u32[]{:S(2)}, u32[]{:S(2)}) collective-permute-start(bf16[2,8,2,64,256]{4,3,2,1,0:T(8,128)(2,1)S(1)} %arrange_factors.1.refs_1_), channel_id=1, source_target_pairs={{0,1},{1,2},{2,3},{3,0},{4,5},{5,6},{6,7},{7,4},{8,9},{9,10},{10,1... | collective-permute-start | bytes 3145736 | tf_op jit(solution)/shard_map/ppermute | solution.py:285
  6.4 3.2 %collective-permute-start.2 = (bf16[2,8,2,64,256]{4,3,2,1,0:T(8,128)(2,1)S(1)}, bf16[2,8,2,64,256]{4,3,2,1,0:T(8,128)(2,1)}, u32[]{:S(2)}, u32[]{:S(2)}) collective-permute-start(bf16[2,8,2,64,256]{4,3,2,1,0:T(8,128)(2,1)S(1)} %arrange_factors.1.refs_1_), channel_id=1, source_target_pairs={{0,3},{1,0},{2,1},{3,2},{4,7},{5,4},{6,5},{7,6},{8,11},{9,8},{10,9... | collective-permute-start | bytes 3145736 | tf_op jit(solution)/shard_map/ppermute | solution.py:286
  9.6 0.0 copy-start.4
  9.7 0.0 copy-start.5
  9.7 0.0 copy-done.6
  9.7 0.6 copy-done.4
  10.3 0.0 copy-done.5
  10.3 0.0 copy-start.2
  10.3 1.2 %copy-done.2 = bf16[16,8,4096]{2,1,0:T(8,128)(2,1)S(1)} copy-done((bf16[16,8,4096]{2,1,0:T(8,128)(2,1)S(1)}, bf16[16,8,4096]{2,1,0:T(8,128)(2,1)}, u32[]{:S(2)}) %copy-start.2) | copy-done | bytes 1048600
  11.6 1.9 %pack_tiles.1 = (bf16[16,144,128]{2,1,0:T(8,128)(2,1)}, s32[16]{0:T(128)S(1)}) custom-call(s32[1]{0:T(128)} %bitcast.lead_ref, s32[2,16]{1,0:T(2,128)S(1)} %bitcast.15, s32[16]{0:T(128)S(1)} %copy-done.6, s32[128]{0:T(128)S(1)} %copy-done.5, bf16[16,8,4096]{2,1,0:T(8,128)(2,1)S(1)} %copy-done.2), custom_call_target="tpu_custom_call" | custom-call | tf_op jit(solution)/shard_map/pack_tiles/pallas_call | solution.py:114
  13.5 13.8 %all-to-all-start = ((bf16[16,144,128]{2,1,0:T(8,128)(2,1)}), bf16[16,144,128]{2,1,0:T(8,128)(2,1)S(1)}, u32[]{:S(2)}, u32[]{:S(2)}) async-start(bf16[16,144,128]{2,1,0:T(8,128)(2,1)} %get-tuple-element.8), calls=%async_computation | async-start | bytes 1179648 | tf_op jit(solution)/shard_map/all_to_all | solution.py:293
  27.3 0.0 collective-permute-done.refs_2_
  27.3 0.8 %slice.12 = bf16[1,8,2,64,256]{4,3,2,1,0:T(8,128)(2,1)} slice(bf16[2,8,2,64,256]{4,3,2,1,0:T(8,128)(2,1)S(1)} %collective-permute-done.refs_2_), slice={[0:1], [0:8], [0:2], [0:64], [0:256]} | slice | bytes 1048576 | tf_op jit(solution)/shard_map/slice | solution.py:287
  28.2 4.0 %collective-permute-start.1 = (bf16[1,8,2,64,256]{4,3,2,1,0:T(8,128)(2,1)}, bf16[1,8,2,64,256]{4,3,2,1,0:T(8,128)(2,1)S(1)}, u32[]{:S(2)}, u32[]{:S(2)}) collective-permute-start(bf16[1,8,2,64,256]{4,3,2,1,0:T(8,128)(2,1)} %slice.12), channel_id=1, source_target_pairs={{0,1},{1,2},{2,3},{3,0},{4,5},{5,6},{6,7},{7,4},{8,9},{9,10},{10,1... | collective-permute-start | bytes 1572872 | tf_op jit(solution)/shard_map/ppermute | solution.py:287
  32.2 0.0 collective-permute-done.2.refs_3_
  32.2 1.9 %slice.13 = bf16[1,8,2,64,256]{4,3,2,1,0:T(8,128)(2,1)} slice(bf16[2,8,2,64,256]{4,3,2,1,0:T(8,128)(2,1)} %collective-permute-done.2.refs_3_), slice={[1:2], [0:8], [0:2], [0:64], [0:256]} | slice | bytes 1048576 | tf_op jit(solution)/shard_map/slice | solution.py:288
  34.1 4.3 %collective-permute-start.3 = (bf16[1,8,2,64,256]{4,3,2,1,0:T(8,128)(2,1)}, bf16[1,8,2,64,256]{4,3,2,1,0:T(8,128)(2,1)}, u32[]{:S(2)}, u32[]{:S(2)}) collective-permute-start(bf16[1,8,2,64,256]{4,3,2,1,0:T(8,128)(2,1)} %slice.13), channel_id=1, source_target_pairs={{0,3},{1,0},{2,1},{3,2},{4,7},{5,4},{6,5},{7,6},{8,11},{9,8},{10,9... | collective-permute-start | bytes 1572872 | tf_op jit(solution)/shard_map/ppermute | solution.py:288
  38.4 7.6 %all-to-all-done.refs_0_ = bf16[16,144,128]{2,1,0:T(8,128)(2,1)S(1)} async-done(((bf16[16,144,128]{2,1,0:T(8,128)(2,1)}), bf16[16,144,128]{2,1,0:T(8,128)(2,1)S(1)}, u32[]{:S(2)}, u32[]{:S(2)}) %all-to-all-start) | async-done | bytes 589856 | tf_op jit(solution)/shard_map/all_to_all | solution.py:293
  46.0 9.8 %ladder_terms.2.refs_3_ = f32[32,64,128]{2,1,0:T(8,128)S(1)} custom-call(bf16[16,144,128]{2,1,0:T(8,128)(2,1)S(1)} %all-to-all-done.refs_0_, bf16[2,8,2,64,256]{4,3,2,1,0:T(8,128)(2,1)S(1)} %arrange_factors.1.refs_1_, bf16[2,8,2,64,256]{4,3,2,1,0:T(8,128)(2,1)S(1)} %collective-permute-done.refs_2_, bf16[2,8,2,64,256]{4,3,2,1,0:T(8,128)(2,1)} %collective-permute-done.2.refs_3_), custom_call_target="tpu_custom_call" | custom-call | flops 4026531 | bytes 1572864 | tf_op jit(solution)/shard_map/ladder_terms/pallas_call | solution.py:214
  55.8 0.0 collective-permute-done.1.refs_1_
  55.8 0.0 collective-permute-done.3.refs_2_
  55.8 6.0 %ladder_terms.3 = bf16[32,64,128]{2,1,0:T(8,128)(2,1)} custom-call(bf16[16,144,128]{2,1,0:T(8,128)(2,1)S(1)} %all-to-all-done.refs_0_, bf16[1,8,2,64,256]{4,3,2,1,0:T(8,128)(2,1)S(1)} %collective-permute-done.1.refs_1_, bf16[1,8,2,64,256]{4,3,2,1,0:T(8,128)(2,1)} %collective-permute-done.3.refs_2_, f32[32,64,128]{2,1,0:T(8,128)S(1)} %ladder_terms.2.refs_3_), custom_call_target="tpu_custom_call" | custom-call | flops 2684354 | bytes 1048576 | tf_op jit(solution)/shard_map/ladder_terms/pallas_call | solution.py:214
  61.8 0.0 copy-start.3
  61.8 3.6 %all-to-all-start.1 = ((bf16[32,64,128]{2,1,0:T(8,128)(2,1)}), bf16[32,64,128]{2,1,0:T(8,128)(2,1)S(1)}, u32[]{:S(2)}, u32[]{:S(2)}) async-start(bf16[32,64,128]{2,1,0:T(8,128)(2,1)} %ladder_terms.3), calls=%async_computation.1 | async-start | bytes 1048576 | tf_op jit(solution)/shard_map/all_to_all | solution.py:297
  65.5 0.0 copy-done
  65.5 0.2 convolution_bitcast_fusion.1
  65.7 0.1 broadcast_and_fusion
  65.8 0.0 copy-done.3
  65.8 0.8 convolution_bitcast_fusion
  66.6 0.4 copy.8.cycle_ref
  67.0 15.7 %all-to-all-done.1.returned_ref = bf16[32,64,128]{2,1,0:T(8,128)(2,1)S(1)} async-done(((bf16[32,64,128]{2,1,0:T(8,128)(2,1)}), bf16[32,64,128]{2,1,0:T(8,128)(2,1)S(1)}, u32[]{:S(2)}, u32[]{:S(2)}) %all-to-all-start.1) | async-done | bytes 524320 | tf_op jit(solution)/shard_map/all_to_all | solution.py:297
  82.7 1.6 %finish_tiles.1 = bf16[16,2,4096]{2,1,0:T(2,128)(2,1)} custom-call(s32[16]{0:T(128)S(1)} %get-tuple-element.7.slot_ref, bf16[32,64,128]{2,1,0:T(8,128)(2,1)S(1)} %all-to-all-done.1.returned_ref, f32[16,2,4096]{2,1,0:T(2,128)S(1)} %copy.8.cycle_ref), custom_call_target="tpu_custom_call" | custom-call | tf_op jit(solution)/shard_map/finish_tiles/pallas_call | solution.py:247
  (3 shorter events, 0.0 us)
Async XLA Ops:
  0.0 65.5 %copy-start = (bf16[64,8,8]{0,2,1:T(8,128)(2,1)S(1)}, bf16[64,8,8]{0,2,1:T(8,128)(2,1)}, u32[]{:S(2)}) copy-start(bf16[64,8,8]{0,2,1:T(8,128)(2,1)} %param.10) | copy-start | bytes 24580
  0.0 1.2 %copy-start.1 = (bf16[8,2,8,4096]{3,2,1,0:T(8,128)(2,1)S(1)}, bf16[8,2,8,4096]{3,2,1,0:T(8,128)(2,1)}, u32[]{:S(2)}) copy-start(bf16[8,2,8,4096]{3,2,1,0:T(8,128)(2,1)} %factor_ref.1) | copy-start | bytes 3145732
  1.2 8.4 %copy-start.6 = (s32[16]{0:T(128)S(1)}, s32[16]{0:T(128)}, u32[]{:S(2)}) copy-start(s32[16]{0:T(128)} %live_ref.1) | copy-start | bytes 196
  2.5 24.8 %collective-permute-start = (bf16[2,8,2,64,256]{4,3,2,1,0:T(8,128)(2,1)S(1)}, bf16[2,8,2,64,256]{4,3,2,1,0:T(8,128)(2,1)S(1)}, u32[]{:S(2)}, u32[]{:S(2)}) collective-permute-start(bf16[2,8,2,64,256]{4,3,2,1,0:T(8,128)(2,1)S(1)} %arrange_factors.1.refs_1_), channel_id=1, source_target_pairs={{0,1},{1,2},{2,3},{3,0},{4,5},{5,6},{6,7},{7,4},{8,9},{9,10},{10,1... | collective-permute-start | bytes 3145736 | tf_op jit(solution)/shard_map/ppermute | solution.py:285
  6.4 25.8 %collective-permute-start.2 = (bf16[2,8,2,64,256]{4,3,2,1,0:T(8,128)(2,1)S(1)}, bf16[2,8,2,64,256]{4,3,2,1,0:T(8,128)(2,1)}, u32[]{:S(2)}, u32[]{:S(2)}) collective-permute-start(bf16[2,8,2,64,256]{4,3,2,1,0:T(8,128)(2,1)S(1)} %arrange_factors.1.refs_1_), channel_id=1, source_target_pairs={{0,3},{1,0},{2,1},{3,2},{4,7},{5,4},{6,5},{7,6},{8,11},{9,8},{10,9... | collective-permute-start | bytes 3145736 | tf_op jit(solution)/shard_map/ppermute | solution.py:286
  9.6 0.7 copy-start.4
  9.7 0.7 copy-start.5
  10.3 1.2 %copy-start.2 = (bf16[16,8,4096]{2,1,0:T(8,128)(2,1)S(1)}, bf16[16,8,4096]{2,1,0:T(8,128)(2,1)}, u32[]{:S(2)}) copy-start(bf16[16,8,4096]{2,1,0:T(8,128)(2,1)} %amp_ref.1) | copy-start | bytes 3145732
  13.5 32.5 %all-to-all-start = ((bf16[16,144,128]{2,1,0:T(8,128)(2,1)}), bf16[16,144,128]{2,1,0:T(8,128)(2,1)S(1)}, u32[]{:S(2)}, u32[]{:S(2)}) async-start(bf16[16,144,128]{2,1,0:T(8,128)(2,1)} %get-tuple-element.8), calls=%async_computation | async-start | bytes 1179648 | tf_op jit(solution)/shard_map/all_to_all | solution.py:293
  28.2 27.6 %collective-permute-start.1 = (bf16[1,8,2,64,256]{4,3,2,1,0:T(8,128)(2,1)}, bf16[1,8,2,64,256]{4,3,2,1,0:T(8,128)(2,1)S(1)}, u32[]{:S(2)}, u32[]{:S(2)}) collective-permute-start(bf16[1,8,2,64,256]{4,3,2,1,0:T(8,128)(2,1)} %slice.12), channel_id=1, source_target_pairs={{0,1},{1,2},{2,3},{3,0},{4,5},{5,6},{6,7},{7,4},{8,9},{9,10},{10,1... | collective-permute-start | bytes 1572872 | tf_op jit(solution)/shard_map/ppermute | solution.py:287
  34.1 21.7 %collective-permute-start.3 = (bf16[1,8,2,64,256]{4,3,2,1,0:T(8,128)(2,1)}, bf16[1,8,2,64,256]{4,3,2,1,0:T(8,128)(2,1)}, u32[]{:S(2)}, u32[]{:S(2)}) collective-permute-start(bf16[1,8,2,64,256]{4,3,2,1,0:T(8,128)(2,1)} %slice.13), channel_id=1, source_target_pairs={{0,3},{1,0},{2,1},{3,2},{4,7},{5,4},{6,5},{7,6},{8,11},{9,8},{10,9... | collective-permute-start | bytes 1572872 | tf_op jit(solution)/shard_map/ppermute | solution.py:288
  61.8 4.0 %copy-start.3 = (bf16[16,8,4096]{2,1,0:T(8,128)(2,1)S(1)}, bf16[16,8,4096]{2,1,0:T(8,128)(2,1)}, u32[]{:S(2)}) copy-start(bf16[16,8,4096]{2,1,0:T(8,128)(2,1)} %amp_ref.1) | copy-start | bytes 3145732
  61.8 20.8 %all-to-all-start.1 = ((bf16[32,64,128]{2,1,0:T(8,128)(2,1)}), bf16[32,64,128]{2,1,0:T(8,128)(2,1)S(1)}, u32[]{:S(2)}, u32[]{:S(2)}) async-start(bf16[32,64,128]{2,1,0:T(8,128)(2,1)} %ladder_terms.3), calls=%async_computation.1 | async-start | bytes 1048576 | tf_op jit(solution)/shard_map/all_to_all | solution.py:297

commit v2 on v1

--- a/solution.py
+++ b/solution.py
@@ -10,7 +10,12 @@
 GROUP = 4
 LANES = 128
 LABEL_ROWS = 16
-UNROLL = 8
+FAR_UP = 9
+CHUNK = 4
+UNROLL = 16
+PIECE = 16
+OUT_SLOTS = 8
+PACK_VMEM = 57 * 1024 * 1024
 SMALL_VMEM = 16 * 1024 * 1024
 LADDER_VMEM = 40 * 1024 * 1024
 
@@ -44,13 +49,13 @@
                     even, odd = join(rows[2 * pair], rows[2 * pair + 1])
                     lanes = slice(pair * LANES, (pair + 1) * LANES)
                     if side == 0:
-                        out_ref[half, v, 0, 0:32, lanes] = even.astype(jnp.bfloat16)
-                        out_ref[half, v, 0, 32:64, lanes] = odd.astype(jnp.bfloat16)
+                        out_ref[2 * v + half, 0, 0:32, lanes] = even.astype(jnp.bfloat16)
+                        out_ref[2 * v + half, 0, 32:64, lanes] = odd.astype(jnp.bfloat16)
                     else:
                         spot = half * 2 + pair
                         woven[spot, pl.ds(0, 32, stride=2), :] = even
                         woven[spot, pl.ds(1, 32, stride=2), :] = odd
-                        out_ref[half, v, 1, :, lanes] = woven[spot].astype(jnp.bfloat16)
+                        out_ref[2 * v + half, 1, :, lanes] = woven[spot].astype(jnp.bfloat16)
         return carry
 
     lax.fori_loop(0, factor_ref.shape[0], one, 0)
@@ -60,7 +65,7 @@
     owned = factors.shape[0]
     return pl.pallas_call(
         factor_kernel,
-        out_shape=jax.ShapeDtypeStruct((2, owned, 2, VB, GROUP * VB), jnp.bfloat16),
+        out_shape=jax.ShapeDtypeStruct((2 * owned, 2, VB, GROUP * VB), jnp.bfloat16),
         in_specs=[pl.BlockSpec(memory_space=pltpu.VMEM)],
         out_specs=pl.BlockSpec(memory_space=pltpu.VMEM),
         scratch_shapes=[
@@ -73,17 +78,35 @@
 
 
 def pack_kernel(
-    lead_ref, blocks_ref, live_ref, owner_ref, amp_ref, out_ref, slot_ref, counts, labels, scratch, woven
+    lead_ref, blocks_hbm, live_hbm, owner_hbm, amp_hbm, out_ref, slot_ref,
+    blocks_ref, live_ref, owner_ref, amp_ref, counts, labels, scratch, woven, sems,
 ):
+    tables = [
+        pltpu.make_async_copy(source, place, sems.at[k])
+        for k, (source, place) in enumerate(
+            ((blocks_hbm, blocks_ref), (live_hbm, live_ref), (owner_hbm, owner_ref))
+        )
+    ]
+    tiles = amp_ref.shape[0]
+    parts = [
+        pltpu.make_async_copy(amp_hbm.at[pl.ds(k, CHUNK)], amp_ref.at[pl.ds(k, CHUNK)], sems.at[3 + k // CHUNK])
+        for k in range(0, tiles, CHUNK)
+    ]
+    for copy in tables + parts:
+        copy.start()
     peers = out_ref.shape[0]
-    owned = owner_ref.shape[0] // peers
     for s in range(peers):
         counts[s] = 0
         for r in range(CAP):
             labels[s, r] = 0
     out_ref[...] = jnp.zeros(out_ref.shape, out_ref.dtype)
+    for copy in tables:
+        copy.wait()
+    owned = owner_ref.shape[0] // peers
     lead = lead_ref[0]
-    for k in range(amp_ref.shape[0]):
+    for k in range(tiles):
+        if k % CHUNK == 0:
+            parts[k // CHUNK].wait()
         place = owner_ref[blocks_ref[1, k]]
         target = place // owned
         rank = counts[target]
@@ -111,21 +134,27 @@
     tiles = amplitudes.shape[0]
     smem = pl.BlockSpec(memory_space=pltpu.SMEM)
     vmem = pl.BlockSpec(memory_space=pltpu.VMEM)
+    hbm = pl.BlockSpec(memory_space=pltpu.HBM)
     return pl.pallas_call(
         pack_kernel,
         out_shape=(
             jax.ShapeDtypeStruct((peers, CAP * VB + LABEL_ROWS, LANES), jnp.bfloat16),
             jax.ShapeDtypeStruct((tiles,), jnp.int32),
         ),
-        in_specs=[smem, smem, smem, smem, vmem],
+        in_specs=[smem, hbm, hbm, hbm, hbm],
         out_specs=(vmem, smem),
         scratch_shapes=[
+            pltpu.SMEM(tile_blocks.shape, jnp.int32),
+            pltpu.SMEM(live_rows.shape, jnp.int32),
+            pltpu.SMEM(block_owner.shape, jnp.int32),
+            pltpu.VMEM(amplitudes.shape, amplitudes.dtype),
             pltpu.SMEM((peers,), jnp.int32),
             pltpu.SMEM((peers, CAP), jnp.int32),
             pltpu.VMEM((2, 256, LANES), jnp.float32),
             pltpu.VMEM((2, VB, LANES), jnp.float32),
+            pltpu.SemaphoreType.DMA((3 + tiles // CHUNK,)),
         ],
-        compiler_params=pltpu.CompilerParams(vmem_limit_bytes=SMALL_VMEM),
+        compiler_params=pltpu.CompilerParams(vmem_limit_bytes=PACK_VMEM),
         name="pack_tiles",
     )(lead, tile_blocks, live_rows, block_owner, amplitudes)
 
@@ -141,7 +170,7 @@
     copy.wait()
 
 
-def slot_terms(i, label_smem, buffer, halves):
+def slot_terms(i, label_smem, buffer, held):
     peer, rank = i // CAP, i % CAP
     v = label_smem[rank, peer]
     tile = buffer[peer, pl.ds(pl.multiple_of(rank * VB, VB), VB), :].astype(jnp.float32)
@@ -151,8 +180,8 @@
     lower = [jnp.where(low, 0.0, rows).astype(jnp.bfloat16) for rows in (turned, tile)]
     pairs = jnp.concatenate([jnp.concatenate(upper, axis=1), jnp.concatenate(lower, axis=1)], axis=0)
     total = None
-    for h in range(halves.shape[0]):
-        left = halves[h, v, 0]
+    for h, half in [(h, half) for h in range(held.shape[0]) for half in range(2)]:
+        left = held[h, 2 * v + half, 0]
         left = jnp.concatenate([left[:, :LANES], left[:, LANES:]], axis=0)
         middle = jnp.dot(left, pairs, preferred_element_type=jnp.float32).astype(jnp.bfloat16)
         rows = [
@@ -164,7 +193,7 @@
         ]
         term = lax.dot_general(
             jnp.concatenate(rows, axis=0),
-            halves[h, v, 1],
+            held[h, 2 * v + half, 1],
             (((1,), (1,)), ((), ())),
             preferred_element_type=jnp.float32,
         )
@@ -176,58 +205,76 @@
     return jnp.concatenate(flat, axis=0)
 
 
-def ladder_kernel(n, more, *refs):
-    buffer_ref, half_refs = refs[0], refs[1 : 1 + n]
-    earlier_ref = refs[1 + n] if more else None
-    out_ref, buffer, halves, label_vmem, label_smem, sems, label_sem = refs[1 + n + more :]
-    arrive = pltpu.make_async_copy(buffer_ref, buffer, sems.at[n])
-    arrive.start()
-    each = halves.shape[0] // n
-    copies = [
-        pltpu.make_async_copy(half_refs[h], halves.at[pl.ds(h * each, each)], sems.at[h]) for h in range(n)
-    ]
+def ladder_kernel(places, more, buffer, *refs):
+    n = len(places)
+    sources, earlier_ref = refs[:n], refs[n] if more else None
+    out_ref, held, label_vmem, label_smem, sems, label_sem = refs[n + more : 6 + n + more]
+    copies = []
+    for source, (h, first) in zip(sources, places):
+        for begin in range(0, source.shape[0], PIECE):
+            count = min(PIECE, source.shape[0] - begin)
+            copies.append(
+                pltpu.make_async_copy(
+                    source.at[pl.ds(begin, count)], held.at[h, pl.ds(first + begin, count)], sems.at[len(copies)]
+                )
+            )
     for copy in copies:
         copy.start()
-    arrive.wait()
     read_labels(buffer, label_vmem, label_smem, label_sem)
     for copy in copies:
         copy.wait()
 
-    def some(j, carry):
-        for k in range(UNROLL):
-            i = j * UNROLL + k
-            terms = slot_terms(i, label_smem, buffer, halves)
-            if more:
-                terms = terms + earlier_ref[i]
-            out_ref[i] = terms.astype(out_ref.dtype)
-        return carry
-
-    lax.fori_loop(0, out_ref.shape[0] // UNROLL, some, 0)
-
-
-def ladder_terms(buffer, halves, earlier=None):
-    peers = buffer.shape[0]
-    slots = peers * CAP
-    n, more = len(halves), int(earlier is not None)
+    if not more:
+
+        def some(j, carry):
+            for k in range(UNROLL):
+                i = j * UNROLL + k
+                out_ref[i] = slot_terms(i, label_smem, buffer, held)
+            return carry
+
+        lax.fori_loop(0, out_ref.shape[0] // UNROLL, some, 0)
+        return
+
+    done, out_sems = refs[6 + n + more :]
+    slots = done.shape[0]
+    outs = [
+        pltpu.make_async_copy(done.at[pl.ds(k, OUT_SLOTS)], out_ref.at[pl.ds(k, OUT_SLOTS)], out_sems.at[k // OUT_SLOTS])
+        for k in range(0, slots, OUT_SLOTS)
+    ]
+    for i in range(slots):
+        done[i] = (slot_terms(i, label_smem, buffer, held) + earlier_ref[i]).astype(done.dtype)
+        if i % OUT_SLOTS == OUT_SLOTS - 1:
+            outs[i // OUT_SLOTS].start()
+    for copy in outs:
+        copy.wait()
+
+
+def ladder_terms(buffer, factors, places, earlier=None):
+    slots = buffer.shape[0] * CAP
+    n, more = len(factors), int(earlier is not None)
+    shards = 1 + max(h for h, first in places)
+    pieces = max(first + f.shape[0] for f, (h, first) in zip(factors, places))
     vmem, anywhere = pl.BlockSpec(memory_space=pltpu.VMEM), pl.BlockSpec(memory_space=pl.ANY)
-    passes = slots * n * 2 * 2 * 2 * VB * VB * LANES
+    scratch = [
+        pltpu.VMEM((shards, pieces) + factors[0].shape[1:], factors[0].dtype),
+        pltpu.VMEM((LABEL_ROWS, LANES), jnp.int32),
+        pltpu.SMEM((LABEL_ROWS, LANES), jnp.int32),
+        pltpu.SemaphoreType.DMA((sum(-(-f.shape[0] // PIECE) for f in factors),)),
+        pltpu.SemaphoreType.DMA,
+    ]
+    if more:
+        scratch.append(pltpu.VMEM((slots, VB, LANES), jnp.bfloat16))
+        scratch.append(pltpu.SemaphoreType.DMA((slots // OUT_SLOTS,)))
     return pl.pallas_call(
-        lambda *refs: ladder_kernel(n, more, *refs),
+        lambda *refs: ladder_kernel(places, more, *refs),
         out_shape=jax.ShapeDtypeStruct((slots, VB, LANES), jnp.bfloat16 if more else jnp.float32),
-        in_specs=[anywhere] * (1 + n) + [vmem] * more,
-        out_specs=vmem,
-        scratch_shapes=[
-            pltpu.VMEM(buffer.shape, buffer.dtype),
-            pltpu.VMEM((n * halves[0].shape[0],) + halves[0].shape[1:], halves[0].dtype),
-            pltpu.VMEM((LABEL_ROWS, LANES), jnp.int32),
-            pltpu.SMEM((LABEL_ROWS, LANES), jnp.int32),
-            pltpu.SemaphoreType.DMA((n + 1,)),
-            pltpu.SemaphoreType.DMA,
-        ],
+        in_specs=[vmem] + [anywhere] * n + [vmem] * more,
+        out_specs=anywhere if more else vmem,
+        scratch_shapes=scratch,
         compiler_params=pltpu.CompilerParams(vmem_limit_bytes=LADDER_VMEM),
-        cost_estimate=pl.CostEstimate(flops=passes // 100, bytes_accessed=n << 19, transcendentals=0),
+        cost_estimate=pl.CostEstimate(flops=10**7, bytes_accessed=shards << 20, transcendentals=0),
         name="ladder_terms",
-    )(buffer, *halves, *([earlier] if more else []))
+    )(buffer, *factors, *([earlier] if more else []))
 
 
 def finish_kernel(slot_ref, returned_ref, cycle_ref, out_ref, scratch):
@@ -284,16 +331,16 @@
     own = arrange_factors(ladder_factors)
     below = lax.ppermute(own, "rep", up)
     above = lax.ppermute(own, "rep", down)
-    far_first = lax.ppermute(below[0:1], "rep", up)
-    far_second = lax.ppermute(above[1:2], "rep", down)
+    far_first = lax.ppermute(below[:FAR_UP], "rep", up)
+    far_second = lax.ppermute(above[FAR_UP:], "rep", down)
 
     packed, slot = pack(
         lead.astype(jnp.int32).reshape(1), tile_blocks.T, live_rows, block_owner, amplitudes, peers
     )
     buffer = lax.all_to_all(packed, "tile", split_axis=0, concat_axis=0, tiled=True)
     cycle = cycle_terms(lead, share, amplitudes, tile_blocks, live_rows, cycle_coupling)
-    earlier = ladder_terms(buffer, (own, below, above))
-    terms = ladder_terms(buffer, (far_first, far_second), earlier)
+    earlier = ladder_terms(buffer, (own, below, above), ((0, 0), (1, 0), (2, 0)))
+    terms = ladder_terms(buffer, (far_first, far_second), ((0, 0), (0, FAR_UP)), earlier)
     returned = lax.all_to_all(terms, "tile", split_axis=0, concat_axis=0, tiled=True)
     return finish(slot, returned, cycle)
 

time: 85 us -> 82.1 us (0.966)
  waiting for transfers between devices: 23.3 us -> 20.8 us
  starting transfers between devices: 32.9 us -> 35.2 us
  Pallas kernels: 20.6 us -> 18.6 us
    pallas_call x3, Pallas kernels: 17.1 us -> 14.6 us  [the longest x2 13.3 us: ladder_terms(): pl.pallas_call(lambda *refs: ladder_kernel(places, more, *refs), out_shap...]
    ppermute x2, starting transfers between devices: 8.3 us -> 9.69 us  [the longest x1 5.42 us: local(): far_first = lax.ppermute(below[:FAR_UP], 'rep', up)]
    all_to_all x1, waiting for transfers between devices: 7.58 us -> 6.19 us  [local(): lax.all_to_all(packed, 'tile', split_axis=0, concat_axis=0, tiled=True)]
    all_to_all x1, waiting for transfers between devices: 15.7 us -> 14.6 us  [local(): lax.all_to_all(terms, 'tile', split_axis=0, concat_axis=0, tiled=True)]
    all_to_all x1, starting transfers between devices: 3.61 us -> 4.52 us  [local(): lax.all_to_all(terms, 'tile', split_axis=0, concat_axis=0, tiled=True)]
    unnamed x14 -> x12, local copies, waits for them, and re-layouts: 3.14 us -> 2.39 us
where the time goes in v2:
time: 82.1 us; the launch traced here: 81.3 us
  starting transfers between devices  35.2 us (43%)
  waiting for transfers between devices  20.8 us (25%)
  Pallas kernels  18.6 us (23%)
  local copies, waits for them, and re-layouts  5.53 us (7%)
  matrix products  0.98 us (1%)
    all_to_all x1, waiting for transfers between devices, local(): lax.all_to_all(terms, 'tile', split_axis=0, concat_axis=0, tiled=True)  14.6 us
    all_to_all x1, starting transfers between devices, local(): lax.all_to_all(packed, 'tile', split_axis=0, concat_axis=0, tiled=True)  13.8 us
    pallas_call x2, Pallas kernels, ladder_terms(): pl.pallas_call(lambda *refs: ladder_kernel(places, more, *refs), out_shap...  13.3 us
    all_to_all x1, waiting for transfers between devices, local(): lax.all_to_all(packed, 'tile', split_axis=0, concat_axis=0, tiled=True)  6.19 us
    ppermute x1, starting transfers between devices, local(): far_first = lax.ppermute(below[:FAR_UP], 'rep', up)  5.42 us
    all_to_all x1, starting transfers between devices, local(): lax.all_to_all(terms, 'tile', split_axis=0, concat_axis=0, tiled=True)  4.52 us
    ppermute x1, starting transfers between devices, local(): far_second = lax.ppermute(above[FAR_UP:], 'rep', down)  4.27 us
    ppermute x1, starting transfers between devices, local(): below = lax.ppermute(own, 'rep', up)  3.95 us
  transfers between devices with their start and end apart: 6, of which 2 were waited for; matrix products, arithmetic and copies ran while one was open for 5% of the time, Pallas kernels for 14%

profile of v2, /device:TPU:1, one launch (start us, length us, event | category | flops | bytes accessed | tf_op | source)
XLA Modules:
  0.0 81.3 jit_solution(11044380518468955990)
XLA Ops:
  0.0 0.0 copy-start
  0.0 0.0 copy-start.1
  0.0 1.2 %copy-done.1 = bf16[8,2,8,4096]{3,2,1,0:T(8,128)(2,1)S(1)} copy-done((bf16[8,2,8,4096]{3,2,1,0:T(8,128)(2,1)S(1)}, bf16[8,2,8,4096]{3,2,1,0:T(8,128)(2,1)}, u32[]{:S(2)}) %copy-start.1) | copy-done | bytes 1048600
  1.2 1.2 %arrange_factors.1.refs_1_ = bf16[16,2,64,256]{3,2,1,0:T(8,128)(2,1)S(1)} custom-call(bf16[8,2,8,4096]{3,2,1,0:T(8,128)(2,1)S(1)} %copy-done.1), custom_call_target="tpu_custom_call" | custom-call | tf_op jit(solution)/shard_map/arrange_factors/pallas_call | solution.py:66
  2.5 3.9 %collective-permute-start = (bf16[16,2,64,256]{3,2,1,0:T(8,128)(2,1)S(1)}, bf16[16,2,64,256]{3,2,1,0:T(8,128)(2,1)S(1)}, u32[]{:S(2)}, u32[]{:S(2)}) collective-permute-start(bf16[16,2,64,256]{3,2,1,0:T(8,128)(2,1)S(1)} %arrange_factors.1.refs_1_), channel_id=1, source_target_pairs={{0,1},{1,2},{2,3},{3,0},{4,5},{5,6},{6,7},{7,4},{8,9},{9,10},{10,1... | collective-permute-start | bytes 3145736 | tf_op jit(solution)/shard_map/ppermute | solution.py:332
  6.4 3.2 %collective-permute-start.2 = (bf16[16,2,64,256]{3,2,1,0:T(8,128)(2,1)S(1)}, bf16[16,2,64,256]{3,2,1,0:T(8,128)(2,1)}, u32[]{:S(2)}, u32[]{:S(2)}) collective-permute-start(bf16[16,2,64,256]{3,2,1,0:T(8,128)(2,1)S(1)} %arrange_factors.1.refs_1_), channel_id=1, source_target_pairs={{0,3},{1,0},{2,1},{3,2},{4,7},{5,4},{6,5},{7,6},{8,11},{9,8},{10,9... | collective-permute-start | bytes 3145736 | tf_op jit(solution)/shard_map/ppermute | solution.py:333
  9.6 2.5 %pack_tiles.1 = (bf16[16,144,128]{2,1,0:T(8,128)(2,1)}, s32[16]{0:T(128)}) custom-call(s32[1]{0:T(128)} %bitcast.lead_ref, s32[2,16]{1,0:T(2,128)} %bitcast.15, s32[16]{0:T(128)} %live_hbm.1, s32[128]{0:T(128)} %owner_hbm.1, bf16[16,8,4096]{2,1,0:T(8,128)(2,1)} %amp_hbm.1), custom_call_target="tpu_custom_call" | custom-call | tf_op jit(solution)/shard_map/pack_tiles/pallas_call | solution.py:138
  12.1 13.8 %all-to-all-start = ((bf16[16,144,128]{2,1,0:T(8,128)(2,1)}), bf16[16,144,128]{2,1,0:T(8,128)(2,1)S(1)}, u32[]{:S(2)}, u32[]{:S(2)}) async-start(bf16[16,144,128]{2,1,0:T(8,128)(2,1)} %get-tuple-element.8), calls=%async_computation | async-start | bytes 1179648 | tf_op jit(solution)/shard_map/all_to_all | solution.py:340
  25.9 0.0 collective-permute-done.refs_2_
  25.9 0.9 %slice.12 = bf16[9,2,64,256]{3,2,1,0:T(8,128)(2,1)} slice(bf16[16,2,64,256]{3,2,1,0:T(8,128)(2,1)S(1)} %collective-permute-done.refs_2_), slice={[0:9], [0:2], [0:64], [0:256]} | slice | bytes 1179648 | tf_op jit(solution)/shard_map/slice | solution.py:334
  26.8 5.4 %collective-permute-start.1 = (bf16[9,2,64,256]{3,2,1,0:T(8,128)(2,1)}, bf16[9,2,64,256]{3,2,1,0:T(8,128)(2,1)S(1)}, u32[]{:S(2)}, u32[]{:S(2)}) collective-permute-start(bf16[9,2,64,256]{3,2,1,0:T(8,128)(2,1)} %slice.12), channel_id=1, source_target_pairs={{0,1},{1,2},{2,3},{3,0},{4,5},{5,6},{6,7},{7,4},{8,9},{9,10},{10,1... | collective-permute-start | bytes 1769480 | tf_op jit(solution)/shard_map/ppermute | solution.py:334
  32.3 0.0 collective-permute-done.2.refs_3_
  32.3 1.8 %slice.13 = bf16[7,2,64,256]{3,2,1,0:T(8,128)(2,1)} slice(bf16[16,2,64,256]{3,2,1,0:T(8,128)(2,1)} %collective-permute-done.2.refs_3_), slice={[9:16], [0:2], [0:64], [0:256]} | slice | bytes 917504 | tf_op jit(solution)/shard_map/slice | solution.py:335
  34.1 4.3 %collective-permute-start.3 = (bf16[7,2,64,256]{3,2,1,0:T(8,128)(2,1)}, bf16[7,2,64,256]{3,2,1,0:T(8,128)(2,1)}, u32[]{:S(2)}, u32[]{:S(2)}) collective-permute-start(bf16[7,2,64,256]{3,2,1,0:T(8,128)(2,1)} %slice.13), channel_id=1, source_target_pairs={{0,3},{1,0},{2,1},{3,2},{4,7},{5,4},{6,5},{7,6},{8,11},{9,8},{10,9... | collective-permute-start | bytes 1376264 | tf_op jit(solution)/shard_map/ppermute | solution.py:335
  38.4 6.2 %all-to-all-done.refs_0_ = bf16[16,144,128]{2,1,0:T(8,128)(2,1)S(1)} async-done(((bf16[16,144,128]{2,1,0:T(8,128)(2,1)}), bf16[16,144,128]{2,1,0:T(8,128)(2,1)S(1)}, u32[]{:S(2)}, u32[]{:S(2)}) %all-to-all-start) | async-done | bytes 589856 | tf_op jit(solution)/shard_map/all_to_all | solution.py:340
  44.6 8.8 %ladder_terms.2.refs_3_ = f32[32,64,128]{2,1,0:T(8,128)S(1)} custom-call(bf16[16,144,128]{2,1,0:T(8,128)(2,1)S(1)} %all-to-all-done.refs_0_, bf16[16,2,64,256]{3,2,1,0:T(8,128)(2,1)S(1)} %arrange_factors.1.refs_1_, bf16[16,2,64,256]{3,2,1,0:T(8,128)(2,1)S(1)} %collective-permute-done.refs_2_, bf16[16,2,64,256]{3,2,1,0:T(8,128)(2,1)} %collective-permute-done.2.refs_3_), custom_call_target="tpu_custom_call" | custom-call | flops 10000000 | bytes 3145728 | tf_op jit(solution)/shard_map/ladder_terms/pallas_call | solution.py:268
  53.4 0.0 collective-permute-done.3.refs_2_
  53.4 0.0 collective-permute-done.1.refs_1_
  53.4 4.5 %ladder_terms.3 = bf16[32,64,128]{2,1,0:T(8,128)(2,1)} custom-call(bf16[16,144,128]{2,1,0:T(8,128)(2,1)S(1)} %all-to-all-done.refs_0_, bf16[9,2,64,256]{3,2,1,0:T(8,128)(2,1)S(1)} %collective-permute-done.1.refs_1_, bf16[7,2,64,256]{3,2,1,0:T(8,128)(2,1)} %collective-permute-done.3.refs_2_, f32[32,64,128]{2,1,0:T(8,128)S(1)} %ladder_terms.2.refs_3_), custom_call_target="tpu_custom_call" | custom-call | flops 10000000 | bytes 1048576 | tf_op jit(solution)/shard_map/ladder_terms/pallas_call | solution.py:268
  57.9 0.0 copy-start.3
  57.9 4.5 %all-to-all-start.1 = ((bf16[32,64,128]{2,1,0:T(8,128)(2,1)}), bf16[32,64,128]{2,1,0:T(8,128)(2,1)S(1)}, u32[]{:S(2)}, u32[]{:S(2)}) async-start(bf16[32,64,128]{2,1,0:T(8,128)(2,1)} %ladder_terms.3), calls=%async_computation.1 | async-start | bytes 1048576 | tf_op jit(solution)/shard_map/all_to_all | solution.py:344
  62.5 0.0 copy-start.4
  62.5 0.7 copy-done.4
  63.1 0.0 copy-done
  63.2 0.0 copy-start.5
  63.2 0.2 convolution_bitcast_fusion.1
  63.3 0.5 copy-done.5
  63.8 0.1 broadcast_and_fusion
  63.9 0.0 copy-done.3
  63.9 0.8 convolution_bitcast_fusion
  64.7 0.4 copy.8.cycle_ref
  65.1 0.0 copy-start.2
  65.1 14.6 %all-to-all-done.1.returned_ref = bf16[32,64,128]{2,1,0:T(8,128)(2,1)S(1)} async-done(((bf16[32,64,128]{2,1,0:T(8,128)(2,1)}), bf16[32,64,128]{2,1,0:T(8,128)(2,1)S(1)}, u32[]{:S(2)}, u32[]{:S(2)}) %all-to-all-start.1) | async-done | bytes 524320 | tf_op jit(solution)/shard_map/all_to_all | solution.py:344
  79.8 0.0 copy-done.2
  79.8 1.6 %finish_tiles.1 = bf16[16,2,4096]{2,1,0:T(2,128)(2,1)} custom-call(s32[16]{0:T(128)S(1)} %copy-done.2, bf16[32,64,128]{2,1,0:T(8,128)(2,1)S(1)} %all-to-all-done.1.returned_ref, f32[16,2,4096]{2,1,0:T(2,128)S(1)} %copy.8.cycle_ref), custom_call_target="tpu_custom_call" | custom-call | tf_op jit(solution)/shard_map/finish_tiles/pallas_call | solution.py:294
  (3 shorter events, 0.0 us)
Async XLA Ops:
  0.0 63.2 %copy-start = (bf16[64,8,8]{0,2,1:T(8,128)(2,1)S(1)}, bf16[64,8,8]{0,2,1:T(8,128)(2,1)}, u32[]{:S(2)}) copy-start(bf16[64,8,8]{0,2,1:T(8,128)(2,1)} %param.10) | copy-start | bytes 24580
  0.0 1.2 %copy-start.1 = (bf16[8,2,8,4096]{3,2,1,0:T(8,128)(2,1)S(1)}, bf16[8,2,8,4096]{3,2,1,0:T(8,128)(2,1)}, u32[]{:S(2)}) copy-start(bf16[8,2,8,4096]{3,2,1,0:T(8,128)(2,1)} %factor_ref.1) | copy-start | bytes 3145732
  2.5 23.4 %collective-permute-start = (bf16[16,2,64,256]{3,2,1,0:T(8,128)(2,1)S(1)}, bf16[16,2,64,256]{3,2,1,0:T(8,128)(2,1)S(1)}, u32[]{:S(2)}, u32[]{:S(2)}) collective-permute-start(bf16[16,2,64,256]{3,2,1,0:T(8,128)(2,1)S(1)} %arrange_factors.1.refs_1_), channel_id=1, source_target_pairs={{0,1},{1,2},{2,3},{3,0},{4,5},{5,6},{6,7},{7,4},{8,9},{9,10},{10,1... | collective-permute-start | bytes 3145736 | tf_op jit(solution)/shard_map/ppermute | solution.py:332
  6.4 25.8 %collective-permute-start.2 = (bf16[16,2,64,256]{3,2,1,0:T(8,128)(2,1)S(1)}, bf16[16,2,64,256]{3,2,1,0:T(8,128)(2,1)}, u32[]{:S(2)}, u32[]{:S(2)}) collective-permute-start(bf16[16,2,64,256]{3,2,1,0:T(8,128)(2,1)S(1)} %arrange_factors.1.refs_1_), channel_id=1, source_target_pairs={{0,3},{1,0},{2,1},{3,2},{4,7},{5,4},{6,5},{7,6},{8,11},{9,8},{10,9... | collective-permute-start | bytes 3145736 | tf_op jit(solution)/shard_map/ppermute | solution.py:333
  12.1 32.5 %all-to-all-start = ((bf16[16,144,128]{2,1,0:T(8,128)(2,1)}), bf16[16,144,128]{2,1,0:T(8,128)(2,1)S(1)}, u32[]{:S(2)}, u32[]{:S(2)}) async-start(bf16[16,144,128]{2,1,0:T(8,128)(2,1)} %get-tuple-element.8), calls=%async_computation | async-start | bytes 1179648 | tf_op jit(solution)/shard_map/all_to_all | solution.py:340
  26.8 26.6 %collective-permute-start.1 = (bf16[9,2,64,256]{3,2,1,0:T(8,128)(2,1)}, bf16[9,2,64,256]{3,2,1,0:T(8,128)(2,1)S(1)}, u32[]{:S(2)}, u32[]{:S(2)}) collective-permute-start(bf16[9,2,64,256]{3,2,1,0:T(8,128)(2,1)} %slice.12), channel_id=1, source_target_pairs={{0,1},{1,2},{2,3},{3,0},{4,5},{5,6},{6,7},{7,4},{8,9},{9,10},{10,1... | collective-permute-start | bytes 1769480 | tf_op jit(solution)/shard_map/ppermute | solution.py:334
  34.1 19.3 %collective-permute-start.3 = (bf16[7,2,64,256]{3,2,1,0:T(8,128)(2,1)}, bf16[7,2,64,256]{3,2,1,0:T(8,128)(2,1)}, u32[]{:S(2)}, u32[]{:S(2)}) collective-permute-start(bf16[7,2,64,256]{3,2,1,0:T(8,128)(2,1)} %slice.13), channel_id=1, source_target_pairs={{0,3},{1,0},{2,1},{3,2},{4,7},{5,4},{6,5},{7,6},{8,11},{9,8},{10,9... | collective-permute-start | bytes 1376264 | tf_op jit(solution)/shard_map/ppermute | solution.py:335
  57.9 6.0 %copy-start.3 = (bf16[16,8,4096]{2,1,0:T(8,128)(2,1)S(1)}, bf16[16,8,4096]{2,1,0:T(8,128)(2,1)}, u32[]{:S(2)}) copy-start(bf16[16,8,4096]{2,1,0:T(8,128)(2,1)} %amp_hbm.1) | copy-start | bytes 3145732
  57.9 21.8 %all-to-all-start.1 = ((bf16[32,64,128]{2,1,0:T(8,128)(2,1)}), bf16[32,64,128]{2,1,0:T(8,128)(2,1)S(1)}, u32[]{:S(2)}, u32[]{:S(2)}) async-start(bf16[32,64,128]{2,1,0:T(8,128)(2,1)} %ladder_terms.3), calls=%async_computation.1 | async-start | bytes 1048576 | tf_op jit(solution)/shard_map/all_to_all | solution.py:344
  62.5 0.7 copy-start.4
  63.2 0.7 copy-start.5
  65.1 14.6 %copy-start.2 = (s32[16]{0:T(128)S(1)}, s32[16]{0:T(128)}, u32[]{:S(2)}) copy-start(s32[16]{0:T(128)} %get-tuple-element.7.slot_ref) | copy-start | bytes 196

commit v3 on v2

--- a/solution.py
+++ b/solution.py
@@ -10,10 +10,9 @@
 GROUP = 4
 LANES = 128
 LABEL_ROWS = 16
-FAR_UP = 9
-CHUNK = 4
-UNROLL = 16
-PIECE = 16
+RELAY_FLOPS = 10**9
+CHUNK = 8
+UNROLL = 32
 OUT_SLOTS = 8
 PACK_VMEM = 57 * 1024 * 1024
 SMALL_VMEM = 16 * 1024 * 1024
@@ -37,44 +36,59 @@
         scratch[t * 8 : (t + 1) * 8, :] = block[:, t * LANES : (t + 1) * LANES]
 
 
-def factor_kernel(factor_ref, out_ref, scratch, woven):
+def factor_kernel(parity_ref, factor_ref, alpha_ref, beta_ref, scratch, woven):
+    parity = parity_ref[0]
+
     def one(v, carry):
         for side in range(2):
             spread_rows(factor_ref[v, side].astype(jnp.float32), scratch.at[side])
-            for half in range(2):
-                rows = [
-                    scratch[side, pl.ds(half * GROUP + q, 32, stride=8), :] for q in range(GROUP)
-                ]
+            for half, out_ref in enumerate((alpha_ref, beta_ref)):
+                begin = ((parity + half) % 2) * GROUP
+                rows = [scratch[side, pl.ds(begin + q, 32, stride=8), :] for q in range(GROUP)]
                 for pair in range(GROUP // 2):
                     even, odd = join(rows[2 * pair], rows[2 * pair + 1])
                     lanes = slice(pair * LANES, (pair + 1) * LANES)
                     if side == 0:
-                        out_ref[2 * v + half, 0, 0:32, lanes] = even.astype(jnp.bfloat16)
-                        out_ref[2 * v + half, 0, 32:64, lanes] = odd.astype(jnp.bfloat16)
+                        turned = jnp.concatenate([even, odd], axis=0).astype(jnp.bfloat16)
                     else:
                         spot = half * 2 + pair
                         woven[spot, pl.ds(0, 32, stride=2), :] = even
                         woven[spot, pl.ds(1, 32, stride=2), :] = odd
-                        out_ref[2 * v + half, 1, :, lanes] = woven[spot].astype(jnp.bfloat16)
+                        turned = woven[spot].astype(jnp.bfloat16)
+                    out_ref[v, side, :, lanes] = turned
         return carry
 
-    lax.fori_loop(0, factor_ref.shape[0], one, 0)
-
-
-def arrange_factors(factors):
+    lax.fori_loop(0, factor_ref.shape[0], one, 0, unroll=4)
+
+
+def arrange_factors(parity, factors):
     owned = factors.shape[0]
     return pl.pallas_call(
         factor_kernel,
-        out_shape=jax.ShapeDtypeStruct((2 * owned, 2, VB, GROUP * VB), jnp.bfloat16),
-        in_specs=[pl.BlockSpec(memory_space=pltpu.VMEM)],
-        out_specs=pl.BlockSpec(memory_space=pltpu.VMEM),
+        out_shape=(jax.ShapeDtypeStruct((owned, 2, VB, GROUP * VB), jnp.bfloat16),) * 2,
+        in_specs=[pl.BlockSpec(memory_space=pltpu.SMEM), pl.BlockSpec(memory_space=pltpu.VMEM)],
+        out_specs=(pl.BlockSpec(memory_space=pltpu.VMEM),) * 2,
         scratch_shapes=[
             pltpu.VMEM((2, 256, LANES), jnp.float32),
             pltpu.VMEM((4, VB, LANES), jnp.float32),
         ],
         compiler_params=pltpu.CompilerParams(vmem_limit_bytes=SMALL_VMEM),
         name="arrange_factors",
-    )(factors)
+    )(parity, factors)
+
+
+def arrived(*pieces):
+    def kernel(*refs):
+        refs[-1][...] = jnp.zeros(refs[-1].shape, refs[-1].dtype)
+
+    return pl.pallas_call(
+        kernel,
+        out_shape=jax.ShapeDtypeStruct((8, LANES), jnp.float32),
+        in_specs=[pl.BlockSpec(memory_space=pl.ANY)] * len(pieces),
+        out_specs=pl.BlockSpec(memory_space=pltpu.VMEM),
+        cost_estimate=pl.CostEstimate(flops=RELAY_FLOPS, bytes_accessed=8, transcendentals=0),
+        name="arrived",
+    )(*pieces)
 
 
 def pack_kernel(
@@ -180,8 +194,8 @@
     lower = [jnp.where(low, 0.0, rows).astype(jnp.bfloat16) for rows in (turned, tile)]
     pairs = jnp.concatenate([jnp.concatenate(upper, axis=1), jnp.concatenate(lower, axis=1)], axis=0)
     total = None
-    for h, half in [(h, half) for h in range(held.shape[0]) for half in range(2)]:
-        left = held[h, 2 * v + half, 0]
+    for h in range(held.shape[0]):
+        left = held[h, v, 0]
         left = jnp.concatenate([left[:, :LANES], left[:, LANES:]], axis=0)
         middle = jnp.dot(left, pairs, preferred_element_type=jnp.float32).astype(jnp.bfloat16)
         rows = [
@@ -193,7 +207,7 @@
         ]
         term = lax.dot_general(
             jnp.concatenate(rows, axis=0),
-            held[h, 2 * v + half, 1],
+            held[h, v, 1],
             (((1,), (1,)), ((), ())),
             preferred_element_type=jnp.float32,
         )
@@ -207,17 +221,14 @@
 
 def ladder_kernel(places, more, buffer, *refs):
     n = len(places)
-    sources, earlier_ref = refs[:n], refs[n] if more else None
-    out_ref, held, label_vmem, label_smem, sems, label_sem = refs[n + more : 6 + n + more]
-    copies = []
-    for source, (h, first) in zip(sources, places):
-        for begin in range(0, source.shape[0], PIECE):
-            count = min(PIECE, source.shape[0] - begin)
-            copies.append(
-                pltpu.make_async_copy(
-                    source.at[pl.ds(begin, count)], held.at[h, pl.ds(first + begin, count)], sems.at[len(copies)]
-                )
-            )
+    sources, earlier_ref = refs[:n], refs[n]
+    out_ref, held, label_vmem, label_smem, sems, label_sem = refs[n + 1 : 7 + n]
+    copies = [
+        pltpu.make_async_copy(
+            source, held.at[pl.ds(h, source.shape[0])] if len(source.shape) > 4 else held.at[h], sems.at[k]
+        )
+        for k, (source, h) in enumerate(zip(sources, places))
+    ]
     for copy in copies:
         copy.start()
     read_labels(buffer, label_vmem, label_smem, label_sem)
@@ -235,7 +246,7 @@
         lax.fori_loop(0, out_ref.shape[0] // UNROLL, some, 0)
         return
 
-    done, out_sems = refs[6 + n + more :]
+    done, out_sems = refs[7 + n :]
     slots = done.shape[0]
     outs = [
         pltpu.make_async_copy(done.at[pl.ds(k, OUT_SLOTS)], out_ref.at[pl.ds(k, OUT_SLOTS)], out_sems.at[k // OUT_SLOTS])
@@ -249,17 +260,18 @@
         copy.wait()
 
 
-def ladder_terms(buffer, factors, places, earlier=None):
+def ladder_terms(buffer, factors, earlier=None, mark=None):
     slots = buffer.shape[0] * CAP
     n, more = len(factors), int(earlier is not None)
-    shards = 1 + max(h for h, first in places)
-    pieces = max(first + f.shape[0] for f, (h, first) in zip(factors, places))
+    last = earlier if more else mark
+    counts = [f.shape[0] if len(f.shape) > 4 else 1 for f in factors]
+    places = [sum(counts[:k]) for k in range(n)]
     vmem, anywhere = pl.BlockSpec(memory_space=pltpu.VMEM), pl.BlockSpec(memory_space=pl.ANY)
     scratch = [
-        pltpu.VMEM((shards, pieces) + factors[0].shape[1:], factors[0].dtype),
+        pltpu.VMEM((sum(counts),) + factors[0].shape[-4:], factors[0].dtype),
         pltpu.VMEM((LABEL_ROWS, LANES), jnp.int32),
         pltpu.SMEM((LABEL_ROWS, LANES), jnp.int32),
-        pltpu.SemaphoreType.DMA((sum(-(-f.shape[0] // PIECE) for f in factors),)),
+        pltpu.SemaphoreType.DMA((n,)),
         pltpu.SemaphoreType.DMA,
     ]
     if more:
@@ -268,35 +280,37 @@
     return pl.pallas_call(
         lambda *refs: ladder_kernel(places, more, *refs),
         out_shape=jax.ShapeDtypeStruct((slots, VB, LANES), jnp.bfloat16 if more else jnp.float32),
-        in_specs=[vmem] + [anywhere] * n + [vmem] * more,
+        in_specs=[vmem] + [anywhere] * n + [vmem if more else anywhere],
         out_specs=anywhere if more else vmem,
         scratch_shapes=scratch,
         compiler_params=pltpu.CompilerParams(vmem_limit_bytes=LADDER_VMEM),
-        cost_estimate=pl.CostEstimate(flops=10**7, bytes_accessed=shards << 20, transcendentals=0),
+        cost_estimate=pl.CostEstimate(flops=10**7, bytes_accessed=sum(counts) << 19, transcendentals=0),
         name="ladder_terms",
-    )(buffer, *factors, *([earlier] if more else []))
+    )(buffer, *factors, last)
 
 
 def finish_kernel(slot_ref, returned_ref, cycle_ref, out_ref, scratch):
-    for k in range(out_ref.shape[0]):
-        spot = k % 2
-        block = returned_ref[slot_ref[k]].astype(jnp.float32)
-        for p in range(2):
-            scratch[spot, pl.ds(p, 32, stride=2), :] = block[p * 32 : (p + 1) * 32]
+    for g in range(out_ref.shape[0] // 4):
+        spot = g % 2
+        for j in range(4):
+            block = returned_ref[slot_ref[4 * g + j]].astype(jnp.float32)
+            for p in range(2):
+                scratch[spot, pl.ds(2 * j + p, 32, stride=8), :] = block[p * 32 : (p + 1) * 32]
         for t in range(32):
             lanes = slice(t * LANES, (t + 1) * LANES)
-            total = scratch[spot, 2 * t : 2 * t + 2, :] + cycle_ref[k, :, lanes]
-            out_ref[k, :, lanes] = total.astype(jnp.bfloat16)
+            total = scratch[spot, 8 * t : 8 * t + 8, :] + cycle_ref[8 * g : 8 * g + 8, lanes]
+            for j in range(4):
+                out_ref[4 * g + j, :, lanes] = total[2 * j : 2 * j + 2].astype(jnp.bfloat16)
 
 
 def finish(slot, returned, cycle):
     vmem = pl.BlockSpec(memory_space=pltpu.VMEM)
     return pl.pallas_call(
         finish_kernel,
-        out_shape=jax.ShapeDtypeStruct(cycle.shape, jnp.bfloat16),
+        out_shape=jax.ShapeDtypeStruct((cycle.shape[0] // 2, 2, cycle.shape[1]), jnp.bfloat16),
         in_specs=[pl.BlockSpec(memory_space=pltpu.SMEM), vmem, vmem],
         out_specs=vmem,
-        scratch_shapes=[pltpu.VMEM((2, VB, LANES), jnp.float32)],
+        scratch_shapes=[pltpu.VMEM((2, 256, LANES), jnp.float32)],
         compiler_params=pltpu.CompilerParams(vmem_limit_bytes=SMALL_VMEM),
         name="finish_tiles",
     )(slot, returned, cycle)
@@ -312,12 +326,11 @@
     mixing = jnp.where(
         same[:, None, :, None] & live[:, None, None, :], coupling[:, :, None, :], 0.0
     ).astype(jnp.bfloat16)
-    cycle = jnp.dot(
+    return jnp.dot(
         mixing.reshape(tiles * share, tiles * rows),
         amplitudes.reshape(tiles * rows, cells),
         preferred_element_type=jnp.float32,
     )
-    return cycle.reshape(tiles, share, cells)
 
 
 def local(amplitudes, tile_blocks, live_rows, ladder_factors, cycle_coupling, block_owner):
@@ -328,19 +341,27 @@
     up = [(i, (i + 1) % reps) for i in range(reps)]
     down = [(i, (i - 1) % reps) for i in range(reps)]
 
-    own = arrange_factors(ladder_factors)
-    below = lax.ppermute(own, "rep", up)
-    above = lax.ppermute(own, "rep", down)
-    far_first = lax.ppermute(below[:FAR_UP], "rep", up)
-    far_second = lax.ppermute(above[FAR_UP:], "rep", down)
+    groups = lax.axis_size("grp")
+    next_group = [(i, (i + 1) % groups) for i in range(groups)]
+    last_group = [(i, (i - 1) % groups) for i in range(groups)]
+    parity = (lax.axis_index("grp") % 2).astype(jnp.int32).reshape(1)
+
+    alpha, beta = arrange_factors(parity, ladder_factors)
+    below_beta = lax.ppermute(beta, "rep", up)
+    above_alpha = lax.ppermute(alpha, "rep", down)
+    far_beta = lax.ppermute(below_beta, "rep", up)
+    far_alpha = lax.ppermute(above_alpha, "rep", down)
+    below_alpha = lax.ppermute(below_beta, "grp", next_group)
+    above_beta = lax.ppermute(above_alpha, "grp", last_group)
 
     packed, slot = pack(
         lead.astype(jnp.int32).reshape(1), tile_blocks.T, live_rows, block_owner, amplitudes, peers
     )
     buffer = lax.all_to_all(packed, "tile", split_axis=0, concat_axis=0, tiled=True)
+    earlier = ladder_terms(buffer, (alpha, beta, below_beta, above_alpha, far_beta, far_alpha), mark=arrived(far_beta, far_alpha))
+    terms = ladder_terms(buffer, (below_alpha, above_beta), earlier)
+    tile_blocks, live_rows, terms = lax.optimization_barrier((tile_blocks, live_rows, terms))
     cycle = cycle_terms(lead, share, amplitudes, tile_blocks, live_rows, cycle_coupling)
-    earlier = ladder_terms(buffer, (own, below, above), ((0, 0), (1, 0), (2, 0)))
-    terms = ladder_terms(buffer, (far_first, far_second), ((0, 0), (0, FAR_UP)), earlier)
     returned = lax.all_to_all(terms, "tile", split_axis=0, concat_axis=0, tiled=True)
     return finish(slot, returned, cycle)
 

time: 82.1 us -> 86.1 us (1.049)
  starting transfers between devices: 35.2 us -> 46.9 us
  waiting for transfers between devices: 20.8 us -> 16.9 us
  local copies, waits for them, and re-layouts: 5.53 us -> 2.77 us
    ppermute x4 -> x6, starting transfers between devices: 16.8 us -> 24.6 us  [the longest x1 9.07 us: local(): above_beta = lax.ppermute(above_alpha, 'grp', last_group)]
    all_to_all x1, waiting for transfers between devices: 6.19 us -> 0.44 us  [local(): lax.all_to_all(packed, 'tile', split_axis=0, concat_axis=0, tiled=True)]
    all_to_all x1, starting transfers between devices: 4.52 us -> 8.48 us  [local(): lax.all_to_all(terms, 'tile', split_axis=0, concat_axis=0, tiled=True)]
    slice x2 -> x0, local copies, waits for them, and re-layouts: 2.73 us -> none  [the longest x1 1.83 us: local(): far_second = lax.ppermute(above[FAR_UP:], 'rep', down)]
    all_to_all x1, waiting for transfers between devices: 14.6 us -> 15.8 us  [local(): lax.all_to_all(terms, 'tile', split_axis=0, concat_axis=0, tiled=True)]
    pallas_call x2 -> x3, Pallas kernels: 2.8 us -> 3.04 us  [the longest x1 1.49 us: finish(): pl.pallas_call(finish_kernel, out_shape=jax.ShapeDtypeStruct((cycle.shape...]
    unnamed x12 -> x14, local copies, waits for them, and re-layouts: 2.39 us -> 2.52 us
  transfers between devices with their start and end apart: 6 -> 8, of which waited for: 2 -> 3; matrix products, arithmetic and copies ran while one was open for 5% -> 1% of each run, Pallas kernels for 14% -> 13%
where the time goes in v3:
time: 86.1 us; the launch traced here: 85.5 us
  starting transfers between devices  46.9 us (54%)
  Pallas kernels  18.1 us (21%)
  waiting for transfers between devices  16.9 us (20%)
  local copies, waits for them, and re-layouts  2.77 us (3%)
    all_to_all x1, waiting for transfers between devices, local(): lax.all_to_all(terms, 'tile', split_axis=0, concat_axis=0, tiled=True)  15.8 us
    all_to_all x1, starting transfers between devices, local(): lax.all_to_all(packed, 'tile', split_axis=0, concat_axis=0, tiled=True)  13.8 us
    pallas_call x2, Pallas kernels, ladder_terms(): pl.pallas_call(lambda *refs: ladder_kernel(places, more, *refs), out_shap...  12.6 us
    ppermute x1, starting transfers between devices, local(): above_beta = lax.ppermute(above_alpha, 'grp', last_group)  9.07 us
    all_to_all x1, starting transfers between devices, local(): lax.all_to_all(terms, 'tile', split_axis=0, concat_axis=0, tiled=True)  8.48 us
    ppermute x1, starting transfers between devices, local(): far_alpha = lax.ppermute(above_alpha, 'rep', down)  4.57 us
    ppermute x1, starting transfers between devices, local(): below_beta = lax.ppermute(beta, 'rep', up)  3.95 us
    ppermute x1, starting transfers between devices, local(): above_alpha = lax.ppermute(alpha, 'rep', down)  3.19 us
  transfers between devices with their start and end apart: 8, of which 3 were waited for; matrix products, arithmetic and copies ran while one was open for 1% of the time, Pallas kernels for 13%

profile of v3, /device:TPU:1, one launch (start us, length us, event | category | flops | bytes accessed | tf_op | source)
XLA Modules:
  0.0 85.5 jit_solution(6361259305452692235)
XLA Ops:
  0.0 0.0 copy-start
  0.0 0.0 copy-start.1
  0.0 1.2 %copy-done.1 = bf16[8,2,8,4096]{3,2,1,0:T(8,128)(2,1)S(1)} copy-done((bf16[8,2,8,4096]{3,2,1,0:T(8,128)(2,1)S(1)}, bf16[8,2,8,4096]{3,2,1,0:T(8,128)(2,1)}, u32[]{:S(2)}) %copy-start.1) | copy-done | bytes 1048600
  1.2 1.0 %arrange_factors.1 = (bf16[8,2,64,256]{3,2,1,0:T(8,128)(2,1)S(1)}, bf16[8,2,64,256]{3,2,1,0:T(8,128)(2,1)S(1)}) custom-call(s32[1]{0:T(128)} %bitcast.2.parity_ref, bf16[8,2,8,4096]{3,2,1,0:T(8,128)(2,1)S(1)} %copy-done.1), custom_call_target="tpu_custom_call" | custom-call | tf_op jit(solution)/shard_map/arrange_factors/pallas_call | solution.py:66
  2.2 3.9 %collective-permute-start = (bf16[8,2,64,256]{3,2,1,0:T(8,128)(2,1)S(1)}, bf16[8,2,64,256]{3,2,1,0:T(8,128)(2,1)S(1)}, u32[]{:S(2)}, u32[]{:S(2)}) collective-permute-start(bf16[8,2,64,256]{3,2,1,0:T(8,128)(2,1)S(1)} %get-tuple-element.14.refs_2_), channel_id=1, source_target_pairs={{0,1},{1,2},{2,3},{3,0},{4,5},{5,6},{6,7},{7,4},{8,9},{9,10},{10,1... | collective-permute-start | bytes 1572872 | tf_op jit(solution)/shard_map/ppermute | solution.py:350
  6.2 3.2 %collective-permute-start.2 = (bf16[8,2,64,256]{3,2,1,0:T(8,128)(2,1)S(1)}, bf16[8,2,64,256]{3,2,1,0:T(8,128)(2,1)}, u32[]{:S(2)}, u32[]{:S(2)}) collective-permute-start(bf16[8,2,64,256]{3,2,1,0:T(8,128)(2,1)S(1)} %get-tuple-element.15.refs_1_), channel_id=1, source_target_pairs={{0,3},{1,0},{2,1},{3,2},{4,7},{5,4},{6,5},{7,6},{8,11},{9,8},{10,9... | collective-permute-start | bytes 1572872 | tf_op jit(solution)/shard_map/ppermute | solution.py:351
  9.4 2.4 %pack_tiles.1 = (bf16[16,144,128]{2,1,0:T(8,128)(2,1)}, s32[16]{0:T(128)}) custom-call(s32[1]{0:T(128)} %bitcast.lead_ref, s32[2,16]{1,0:T(2,128)} %bitcast.16, s32[16]{0:T(128)} %live_hbm.1, s32[128]{0:T(128)} %owner_hbm.1, bf16[16,8,4096]{2,1,0:T(8,128)(2,1)} %amp_hbm.1), custom_call_target="tpu_custom_call" | custom-call | tf_op jit(solution)/shard_map/pack_tiles/pallas_call | solution.py:152
  11.8 13.8 %all-to-all-start = ((bf16[16,144,128]{2,1,0:T(8,128)(2,1)}), bf16[16,144,128]{2,1,0:T(8,128)(2,1)S(1)}, u32[]{:S(2)}, u32[]{:S(2)}) async-start(bf16[16,144,128]{2,1,0:T(8,128)(2,1)} %get-tuple-element.13), calls=%async_computation | async-start | bytes 1179648 | tf_op jit(solution)/shard_map/all_to_all | solution.py:360
  25.6 0.0 collective-permute-done.refs_3_
  25.6 1.9 %collective-permute-start.4 = (bf16[8,2,64,256]{3,2,1,0:T(8,128)(2,1)S(1)}, bf16[8,2,64,256]{3,2,1,0:T(8,128)(2,1)}, u32[]{:S(2)}, u32[]{:S(2)}) collective-permute-start(bf16[8,2,64,256]{3,2,1,0:T(8,128)(2,1)S(1)} %collective-permute-done.refs_3_), channel_id=1, source_target_pairs={{0,1},{1,2},{2,3},{3,0},{4,5},{5,6},{6,7},{7,4},{8,9},{9,10},{10,1... | collective-permute-start | bytes 1572872 | tf_op jit(solution)/shard_map/ppermute | solution.py:352
  27.6 0.0 collective-permute-done.2.refs_4_
  27.6 4.6 %collective-permute-start.5 = (bf16[8,2,64,256]{3,2,1,0:T(8,128)(2,1)}, bf16[8,2,64,256]{3,2,1,0:T(8,128)(2,1)}, u32[]{:S(2)}, u32[]{:S(2)}) collective-permute-start(bf16[8,2,64,256]{3,2,1,0:T(8,128)(2,1)} %collective-permute-done.2.refs_4_), channel_id=1, source_target_pairs={{0,3},{1,0},{2,1},{3,2},{4,7},{5,4},{6,5},{7,6},{8,11},{9,8},{10,9... | collective-permute-start | bytes 1572872 | tf_op jit(solution)/shard_map/ppermute | solution.py:353
  32.1 1.9 %collective-permute-start.1 = (bf16[8,2,64,256]{3,2,1,0:T(8,128)(2,1)S(1)}, bf16[8,2,64,256]{3,2,1,0:T(8,128)(2,1)S(1)}, u32[]{:S(2)}, u32[]{:S(2)}) collective-permute-start(bf16[8,2,64,256]{3,2,1,0:T(8,128)(2,1)S(1)} %collective-permute-done.refs_3_), channel_id=1, source_target_pairs={{0,64},{64,128},{128,192},{192,256},{256,320},{320,384},{384,448},... | collective-permute-start | bytes 1572872 | tf_op jit(solution)/shard_map/ppermute | solution.py:354
  34.1 9.1 %collective-permute-start.3 = (bf16[8,2,64,256]{3,2,1,0:T(8,128)(2,1)}, bf16[8,2,64,256]{3,2,1,0:T(8,128)(2,1)S(1)}, u32[]{:S(2)}, u32[]{:S(2)}) collective-permute-start(bf16[8,2,64,256]{3,2,1,0:T(8,128)(2,1)} %collective-permute-done.2.refs_4_), channel_id=1, source_target_pairs={{0,704},{64,0},{128,64},{192,128},{256,192},{320,256},{384,320},{4... | collective-permute-start | bytes 1572872 | tf_op jit(solution)/shard_map/ppermute | solution.py:355
  43.2 0.0 collective-permute-done.4.refs_0_.refs_5_
  43.2 0.0 collective-permute-done.5.refs_1_.refs_6_
  43.2 0.6 arrived.1.refs_7_
  43.8 0.4 all-to-all-done.refs_0_
  44.3 0.0 copy-start.2
  44.3 0.7 copy-done.2
  45.0 8.5 %ladder_terms.2.refs_3_ = f32[32,64,128]{2,1,0:T(8,128)S(1)} custom-call(bf16[16,144,128]{2,1,0:T(8,128)(2,1)S(1)} %all-to-all-done.refs_0_, bf16[8,2,64,256]{3,2,1,0:T(8,128)(2,1)S(1)} %get-tuple-element.15.refs_1_, bf16[8,2,64,256]{3,2,1,0:T(8,128)(2,1)S(1)} %get-tuple-element.14.refs_2_, bf16[8,2,64,256]{3,2,1,0:T(8,128)(2,1)S(1)} %collective-permute-done.refs_3_, ...), custom_call_target="tpu_custom_call" | custom-call | flops 10000000 | bytes 3145728 | tf_op jit(solution)/shard_map/ladder_terms/pallas_call | solution.py:280
  53.5 0.0 copy-start.6
  53.5 0.0 collective-permute-done.1.refs_1_
  53.5 0.6 collective-permute-done.3.refs_2_
  54.1 4.1 %ladder_terms.3 = bf16[32,64,128]{2,1,0:T(8,128)(2,1)} custom-call(bf16[16,144,128]{2,1,0:T(8,128)(2,1)S(1)} %all-to-all-done.refs_0_, bf16[8,2,64,256]{3,2,1,0:T(8,128)(2,1)S(1)} %collective-permute-done.1.refs_1_, bf16[8,2,64,256]{3,2,1,0:T(8,128)(2,1)S(1)} %collective-permute-done.3.refs_2_, f32[32,64,128]{2,1,0:T(8,128)S(1)} %ladder_terms.2.refs_3_), custom_call_target="tpu_custom_call" | custom-call | flops 10000000 | bytes 1048576 | tf_op jit(solution)/shard_map/ladder_terms/pallas_call | solution.py:280
  58.2 0.0 copy-done.6
  58.2 0.0 copy-start.4
  58.2 8.5 %all-to-all-start.1 = ((bf16[32,64,128]{2,1,0:T(8,128)(2,1)}), bf16[32,64,128]{2,1,0:T(8,128)(2,1)S(1)}, u32[]{:S(2)}, u32[]{:S(2)}) async-start(bf16[32,64,128]{2,1,0:T(8,128)(2,1)} %ladder_terms.3), calls=%async_computation.1 | async-start | bytes 1048576 | tf_op jit(solution)/shard_map/all_to_all | solution.py:365
  66.7 0.0 copy-done
  66.7 0.2 convolution_bitcast_fusion
  66.9 0.0 copy-start.5
  66.9 0.1 copy.8
  67.0 0.6 copy-done.5
  67.5 0.1 iota_compare_fusion.1
  67.6 0.1 broadcast_and_fusion
  67.8 0.2 convert_element_type.15
  67.9 0.0 copy-done.4
  67.9 0.3 fusion.cycle_ref
  68.2 0.0 copy-start.3
  68.2 15.8 %all-to-all-done.1.returned_ref = bf16[32,64,128]{2,1,0:T(8,128)(2,1)S(1)} async-done(((bf16[32,64,128]{2,1,0:T(8,128)(2,1)}), bf16[32,64,128]{2,1,0:T(8,128)(2,1)S(1)}, u32[]{:S(2)}, u32[]{:S(2)}) %all-to-all-start.1) | async-done | bytes 524320 | tf_op jit(solution)/shard_map/all_to_all | solution.py:365
  84.0 0.0 copy-done.3
  84.0 1.5 %finish_tiles.1 = bf16[16,2,4096]{2,1,0:T(2,128)(2,1)} custom-call(s32[16]{0:T(128)S(1)} %copy-done.3, bf16[32,64,128]{2,1,0:T(8,128)(2,1)S(1)} %all-to-all-done.1.returned_ref, f32[32,4096]{1,0:T(8,128)S(1)} %fusion.cycle_ref), custom_call_target="tpu_custom_call" | custom-call | tf_op jit(solution)/shard_map/finish_tiles/pallas_call | solution.py:308
  (3 shorter events, 0.0 us)
Async XLA Ops:
  0.0 66.7 %copy-start = (bf16[64,8,8]{0,2,1:T(8,128)(2,1)S(1)}, bf16[64,8,8]{0,2,1:T(8,128)(2,1)}, u32[]{:S(2)}) copy-start(bf16[64,8,8]{0,2,1:T(8,128)(2,1)} %param.10) | copy-start | bytes 24580
  0.0 1.2 %copy-start.1 = (bf16[8,2,8,4096]{3,2,1,0:T(8,128)(2,1)S(1)}, bf16[8,2,8,4096]{3,2,1,0:T(8,128)(2,1)}, u32[]{:S(2)}) copy-start(bf16[8,2,8,4096]{3,2,1,0:T(8,128)(2,1)} %factor_ref.1) | copy-start | bytes 3145732
  2.2 23.4 %collective-permute-start = (bf16[8,2,64,256]{3,2,1,0:T(8,128)(2,1)S(1)}, bf16[8,2,64,256]{3,2,1,0:T(8,128)(2,1)S(1)}, u32[]{:S(2)}, u32[]{:S(2)}) collective-permute-start(bf16[8,2,64,256]{3,2,1,0:T(8,128)(2,1)S(1)} %get-tuple-element.14.refs_2_), channel_id=1, source_target_pairs={{0,1},{1,2},{2,3},{3,0},{4,5},{5,6},{6,7},{7,4},{8,9},{9,10},{10,1... | collective-permute-start | bytes 1572872 | tf_op jit(solution)/shard_map/ppermute | solution.py:350
  6.2 21.4 %collective-permute-start.2 = (bf16[8,2,64,256]{3,2,1,0:T(8,128)(2,1)S(1)}, bf16[8,2,64,256]{3,2,1,0:T(8,128)(2,1)}, u32[]{:S(2)}, u32[]{:S(2)}) collective-permute-start(bf16[8,2,64,256]{3,2,1,0:T(8,128)(2,1)S(1)} %get-tuple-element.15.refs_1_), channel_id=1, source_target_pairs={{0,3},{1,0},{2,1},{3,2},{4,7},{5,4},{6,5},{7,6},{8,11},{9,8},{10,9... | collective-permute-start | bytes 1572872 | tf_op jit(solution)/shard_map/ppermute | solution.py:351
  11.8 32.5 %all-to-all-start = ((bf16[16,144,128]{2,1,0:T(8,128)(2,1)}), bf16[16,144,128]{2,1,0:T(8,128)(2,1)S(1)}, u32[]{:S(2)}, u32[]{:S(2)}) async-start(bf16[16,144,128]{2,1,0:T(8,128)(2,1)} %get-tuple-element.13), calls=%async_computation | async-start | bytes 1179648 | tf_op jit(solution)/shard_map/all_to_all | solution.py:360
  25.6 17.5 %collective-permute-start.4 = (bf16[8,2,64,256]{3,2,1,0:T(8,128)(2,1)S(1)}, bf16[8,2,64,256]{3,2,1,0:T(8,128)(2,1)}, u32[]{:S(2)}, u32[]{:S(2)}) collective-permute-start(bf16[8,2,64,256]{3,2,1,0:T(8,128)(2,1)S(1)} %collective-permute-done.refs_3_), channel_id=1, source_target_pairs={{0,1},{1,2},{2,3},{3,0},{4,5},{5,6},{6,7},{7,4},{8,9},{9,10},{10,1... | collective-permute-start | bytes 1572872 | tf_op jit(solution)/shard_map/ppermute | solution.py:352
  27.6 15.7 %collective-permute-start.5 = (bf16[8,2,64,256]{3,2,1,0:T(8,128)(2,1)}, bf16[8,2,64,256]{3,2,1,0:T(8,128)(2,1)}, u32[]{:S(2)}, u32[]{:S(2)}) collective-permute-start(bf16[8,2,64,256]{3,2,1,0:T(8,128)(2,1)} %collective-permute-done.2.refs_4_), channel_id=1, source_target_pairs={{0,3},{1,0},{2,1},{3,2},{4,7},{5,4},{6,5},{7,6},{8,11},{9,8},{10,9... | collective-permute-start | bytes 1572872 | tf_op jit(solution)/shard_map/ppermute | solution.py:353
  32.1 21.3 %collective-permute-start.1 = (bf16[8,2,64,256]{3,2,1,0:T(8,128)(2,1)S(1)}, bf16[8,2,64,256]{3,2,1,0:T(8,128)(2,1)S(1)}, u32[]{:S(2)}, u32[]{:S(2)}) collective-permute-start(bf16[8,2,64,256]{3,2,1,0:T(8,128)(2,1)S(1)} %collective-permute-done.refs_3_), channel_id=1, source_target_pairs={{0,64},{64,128},{128,192},{192,256},{256,320},{320,384},{384,448},... | collective-permute-start | bytes 1572872 | tf_op jit(solution)/shard_map/ppermute | solution.py:354
  34.1 20.0 %collective-permute-start.3 = (bf16[8,2,64,256]{3,2,1,0:T(8,128)(2,1)}, bf16[8,2,64,256]{3,2,1,0:T(8,128)(2,1)S(1)}, u32[]{:S(2)}, u32[]{:S(2)}) collective-permute-start(bf16[8,2,64,256]{3,2,1,0:T(8,128)(2,1)} %collective-permute-done.2.refs_4_), channel_id=1, source_target_pairs={{0,704},{64,0},{128,64},{192,128},{256,192},{320,256},{384,320},{4... | collective-permute-start | bytes 1572872 | tf_op jit(solution)/shard_map/ppermute | solution.py:355
  44.3 0.7 copy-start.2
  53.5 4.7 %copy-start.6 = (s32[16,2]{0,1:T(2,128)S(1)}, s32[16,2]{0,1:T(2,128)}, u32[]{:S(2)}) copy-start(s32[16,2]{0,1:T(2,128)} %param.7) | copy-start | bytes 388
  58.2 9.8 %copy-start.4 = (bf16[16,8,4096]{2,1,0:T(8,128)(2,1)S(1)}, bf16[16,8,4096]{2,1,0:T(8,128)(2,1)}, u32[]{:S(2)}) copy-start(bf16[16,8,4096]{2,1,0:T(8,128)(2,1)} %amp_hbm.1) | copy-start | bytes 3145732
  58.2 25.8 %all-to-all-start.1 = ((bf16[32,64,128]{2,1,0:T(8,128)(2,1)}), bf16[32,64,128]{2,1,0:T(8,128)(2,1)S(1)}, u32[]{:S(2)}, u32[]{:S(2)}) async-start(bf16[32,64,128]{2,1,0:T(8,128)(2,1)} %ladder_terms.3), calls=%async_computation.1 | async-start | bytes 1048576 | tf_op jit(solution)/shard_map/all_to_all | solution.py:365
  66.9 0.7 copy-start.5
  68.2 15.8 %copy-start.3 = (s32[16]{0:T(128)S(1)}, s32[16]{0:T(128)}, u32[]{:S(2)}) copy-start(s32[16]{0:T(128)} %get-tuple-element.12.slot_ref) | copy-start | bytes 196

commit v4 on v3

--- a/solution.py
+++ b/solution.py
@@ -36,15 +36,14 @@
         scratch[t * 8 : (t + 1) * 8, :] = block[:, t * LANES : (t + 1) * LANES]
 
 
-def factor_kernel(parity_ref, factor_ref, alpha_ref, beta_ref, scratch, woven):
-    parity = parity_ref[0]
-
+def factor_kernel(factor_ref, both_ref, second_ref, scratch, woven):
     def one(v, carry):
         for side in range(2):
             spread_rows(factor_ref[v, side].astype(jnp.float32), scratch.at[side])
-            for half, out_ref in enumerate((alpha_ref, beta_ref)):
-                begin = ((parity + half) % 2) * GROUP
-                rows = [scratch[side, pl.ds(begin + q, 32, stride=8), :] for q in range(GROUP)]
+            for half in range(2):
+                rows = [
+                    scratch[side, pl.ds(half * GROUP + q, 32, stride=8), :] for q in range(GROUP)
+                ]
                 for pair in range(GROUP // 2):
                     even, odd = join(rows[2 * pair], rows[2 * pair + 1])
                     lanes = slice(pair * LANES, (pair + 1) * LANES)
@@ -55,18 +54,22 @@
                         woven[spot, pl.ds(0, 32, stride=2), :] = even
                         woven[spot, pl.ds(1, 32, stride=2), :] = odd
                         turned = woven[spot].astype(jnp.bfloat16)
-                    out_ref[v, side, :, lanes] = turned
+                    both_ref[half, v, side, :, lanes] = turned
+                    if half == 1:
+                        second_ref[v, side, :, lanes] = turned
         return carry
 
     lax.fori_loop(0, factor_ref.shape[0], one, 0, unroll=4)
 
 
-def arrange_factors(parity, factors):
+def arrange_factors(factors):
     owned = factors.shape[0]
     return pl.pallas_call(
         factor_kernel,
-        out_shape=(jax.ShapeDtypeStruct((owned, 2, VB, GROUP * VB), jnp.bfloat16),) * 2,
-        in_specs=[pl.BlockSpec(memory_space=pltpu.SMEM), pl.BlockSpec(memory_space=pltpu.VMEM)],
+        out_shape=tuple(
+            jax.ShapeDtypeStruct(lead + (owned, 2, VB, GROUP * VB), jnp.bfloat16) for lead in ((2,), ())
+        ),
+        in_specs=[pl.BlockSpec(memory_space=pltpu.VMEM)],
         out_specs=(pl.BlockSpec(memory_space=pltpu.VMEM),) * 2,
         scratch_shapes=[
             pltpu.VMEM((2, 256, LANES), jnp.float32),
@@ -74,21 +77,26 @@
         ],
         compiler_params=pltpu.CompilerParams(vmem_limit_bytes=SMALL_VMEM),
         name="arrange_factors",
-    )(parity, factors)
-
-
-def arrived(*pieces):
-    def kernel(*refs):
-        refs[-1][...] = jnp.zeros(refs[-1].shape, refs[-1].dtype)
-
-    return pl.pallas_call(
-        kernel,
-        out_shape=jax.ShapeDtypeStruct((8, LANES), jnp.float32),
-        in_specs=[pl.BlockSpec(memory_space=pl.ANY)] * len(pieces),
-        out_specs=pl.BlockSpec(memory_space=pltpu.VMEM),
+    )(factors)
+
+
+def relay_kernel(piece_ref, out_ref, sem):
+    copy = pltpu.make_async_copy(piece_ref, out_ref, sem)
+    copy.start()
+    copy.wait()
+
+
+def relay(piece):
+    vmem = pl.BlockSpec(memory_space=pltpu.VMEM)
+    return pl.pallas_call(
+        relay_kernel,
+        out_shape=jax.ShapeDtypeStruct(piece.shape, piece.dtype),
+        in_specs=[vmem],
+        out_specs=vmem,
+        scratch_shapes=[pltpu.SemaphoreType.DMA],
         cost_estimate=pl.CostEstimate(flops=RELAY_FLOPS, bytes_accessed=8, transcendentals=0),
-        name="arrived",
-    )(*pieces)
+        name="relay",
+    )(piece)
 
 
 def pack_kernel(
@@ -221,8 +229,8 @@
 
 def ladder_kernel(places, more, buffer, *refs):
     n = len(places)
-    sources, earlier_ref = refs[:n], refs[n]
-    out_ref, held, label_vmem, label_smem, sems, label_sem = refs[n + 1 : 7 + n]
+    sources, earlier_ref = refs[:n], refs[n] if more else None
+    out_ref, held, label_vmem, label_smem, sems, label_sem = refs[n + more : 6 + n + more]
     copies = [
         pltpu.make_async_copy(
             source, held.at[pl.ds(h, source.shape[0])] if len(source.shape) > 4 else held.at[h], sems.at[k]
@@ -246,7 +254,7 @@
         lax.fori_loop(0, out_ref.shape[0] // UNROLL, some, 0)
         return
 
-    done, out_sems = refs[7 + n :]
+    done, out_sems = refs[6 + n + more :]
     slots = done.shape[0]
     outs = [
         pltpu.make_async_copy(done.at[pl.ds(k, OUT_SLOTS)], out_ref.at[pl.ds(k, OUT_SLOTS)], out_sems.at[k // OUT_SLOTS])
@@ -260,10 +268,9 @@
         copy.wait()
 
 
-def ladder_terms(buffer, factors, earlier=None, mark=None):
+def ladder_terms(buffer, factors, earlier=None):
     slots = buffer.shape[0] * CAP
     n, more = len(factors), int(earlier is not None)
-    last = earlier if more else mark
     counts = [f.shape[0] if len(f.shape) > 4 else 1 for f in factors]
     places = [sum(counts[:k]) for k in range(n)]
     vmem, anywhere = pl.BlockSpec(memory_space=pltpu.VMEM), pl.BlockSpec(memory_space=pl.ANY)
@@ -280,13 +287,13 @@
     return pl.pallas_call(
         lambda *refs: ladder_kernel(places, more, *refs),
         out_shape=jax.ShapeDtypeStruct((slots, VB, LANES), jnp.bfloat16 if more else jnp.float32),
-        in_specs=[vmem] + [anywhere] * n + [vmem if more else anywhere],
+        in_specs=[vmem] + [anywhere] * n + [vmem] * more,
         out_specs=anywhere if more else vmem,
         scratch_shapes=scratch,
         compiler_params=pltpu.CompilerParams(vmem_limit_bytes=LADDER_VMEM),
         cost_estimate=pl.CostEstimate(flops=10**7, bytes_accessed=sum(counts) << 19, transcendentals=0),
         name="ladder_terms",
-    )(buffer, *factors, last)
+    )(buffer, *factors, *([earlier] if more else []))
 
 
 def finish_kernel(slot_ref, returned_ref, cycle_ref, out_ref, scratch):
@@ -341,25 +348,19 @@
     up = [(i, (i + 1) % reps) for i in range(reps)]
     down = [(i, (i - 1) % reps) for i in range(reps)]
 
-    groups = lax.axis_size("grp")
-    next_group = [(i, (i + 1) % groups) for i in range(groups)]
-    last_group = [(i, (i - 1) % groups) for i in range(groups)]
-    parity = (lax.axis_index("grp") % 2).astype(jnp.int32).reshape(1)
-
-    alpha, beta = arrange_factors(parity, ladder_factors)
-    below_beta = lax.ppermute(beta, "rep", up)
-    above_alpha = lax.ppermute(alpha, "rep", down)
-    far_beta = lax.ppermute(below_beta, "rep", up)
-    far_alpha = lax.ppermute(above_alpha, "rep", down)
-    below_alpha = lax.ppermute(below_beta, "grp", next_group)
-    above_beta = lax.ppermute(above_alpha, "grp", last_group)
+    own, second = arrange_factors(ladder_factors)
+    below = lax.ppermute(own, "rep", up)
+    above_second = lax.ppermute(second, "rep", down)
+    far_second = lax.ppermute(relay(above_second), "rep", down)
+    above_first = lax.ppermute(own[0], "rep", down)
+    far_first = lax.ppermute(below[0], "rep", up)
 
     packed, slot = pack(
         lead.astype(jnp.int32).reshape(1), tile_blocks.T, live_rows, block_owner, amplitudes, peers
     )
     buffer = lax.all_to_all(packed, "tile", split_axis=0, concat_axis=0, tiled=True)
-    earlier = ladder_terms(buffer, (alpha, beta, below_beta, above_alpha, far_beta, far_alpha), mark=arrived(far_beta, far_alpha))
-    terms = ladder_terms(buffer, (below_alpha, above_beta), earlier)
+    earlier = ladder_terms(buffer, (own, below, above_second, above_first))
+    terms = ladder_terms(buffer, (far_second, far_first), earlier)
     tile_blocks, live_rows, terms = lax.optimization_barrier((tile_blocks, live_rows, terms))
     cycle = cycle_terms(lead, share, amplitudes, tile_blocks, live_rows, cycle_coupling)
     returned = lax.all_to_all(terms, "tile", split_axis=0, concat_axis=0, tiled=True)

time: 86.1 us -> 86 us (level)
  starting transfers between devices: 46.9 us -> 36.3 us
  waiting for transfers between devices: 16.9 us -> 23.4 us
  Pallas kernels: 18.1 us -> 20.2 us
  local copies, waits for them, and re-layouts: 2.77 us -> 4.55 us
    ppermute x6 -> x5, starting transfers between devices: 24.6 us -> 14.4 us  [the longest x1 3.94 us: local(): below = lax.ppermute(own, 'rep', up)]
    ppermute x6 -> x5, waiting for transfers between devices: 0.64 us -> 5.3 us  [the longest x1 4.62 us: local(): above_first = lax.ppermute(own[0], 'rep', down)]
    pallas_call x2, Pallas kernels: 1.56 us -> 3.52 us  [the longest x1 1.87 us: relay(): pl.pallas_call(relay_kernel, out_shape=jax.ShapeDtypeStruct(piece.shape,...]
    all_to_all x1, waiting for transfers between devices: 0.44 us -> 2.29 us  [local(): lax.all_to_all(packed, 'tile', split_axis=0, concat_axis=0, tiled=True)]
    squeeze x0 -> x2, local copies, waits for them, and re-layouts: none -> 1.68 us  [the longest x1 0.85 us: local(): above_first = lax.ppermute(own[0], 'rep', down)]
    unnamed x14 -> x16, local copies, waits for them, and re-layouts: 2.52 us -> 2.62 us
  transfers between devices with their start and end apart: 8 -> 7, of which waited for: 3 -> 4; matrix products, arithmetic and copies ran while one was open for 1% -> 3% of each run, Pallas kernels for 13% -> 15%
where the time goes in v4:
time: 86 us; the launch traced here: 85.4 us
  starting transfers between devices  36.3 us (42%)
  waiting for transfers between devices  23.4 us (27%)
  Pallas kernels  20.2 us (23%)
  local copies, waits for them, and re-layouts  4.55 us (5%)
    all_to_all x1, waiting for transfers between devices, local(): lax.all_to_all(terms, 'tile', split_axis=0, concat_axis=0, tiled=True)  15.8 us
    all_to_all x1, starting transfers between devices, local(): lax.all_to_all(packed, 'tile', split_axis=0, concat_axis=0, tiled=True)  13.8 us
    pallas_call x2, Pallas kernels, ladder_terms(): pl.pallas_call(lambda *refs: ladder_kernel(places, more, *refs), out_shap...  12.8 us
    all_to_all x1, starting transfers between devices, local(): lax.all_to_all(terms, 'tile', split_axis=0, concat_axis=0, tiled=True)  8.08 us
    ppermute x1, waiting for transfers between devices, local(): above_first = lax.ppermute(own[0], 'rep', down)  4.62 us
    ppermute x1, starting transfers between devices, local(): below = lax.ppermute(own, 'rep', up)  3.94 us
    ppermute x1, starting transfers between devices, local(): far_first = lax.ppermute(below[0], 'rep', up)  3.35 us
    ppermute x1, starting transfers between devices, local(): above_second = lax.ppermute(second, 'rep', down)  3.19 us
  transfers between devices with their start and end apart: 7, of which 4 were waited for; matrix products, arithmetic and copies ran while one was open for 3% of the time, Pallas kernels for 15%

profile of v4, /device:TPU:1, one launch (start us, length us, event | category | flops | bytes accessed | tf_op | source)
XLA Modules:
  0.0 85.4 jit_solution(17666926062864030326)
XLA Ops:
  0.0 0.0 copy-start
  0.0 0.0 copy-start.1
  0.0 1.2 %copy-done.1 = bf16[8,2,8,4096]{3,2,1,0:T(8,128)(2,1)S(1)} copy-done((bf16[8,2,8,4096]{3,2,1,0:T(8,128)(2,1)S(1)}, bf16[8,2,8,4096]{3,2,1,0:T(8,128)(2,1)}, u32[]{:S(2)}) %copy-start.1) | copy-done | bytes 1048600
  1.2 1.7 %arrange_factors.1 = (bf16[2,8,2,64,256]{4,3,2,1,0:T(8,128)(2,1)S(1)}, bf16[8,2,64,256]{3,2,1,0:T(8,128)(2,1)}) custom-call(bf16[8,2,8,4096]{3,2,1,0:T(8,128)(2,1)S(1)} %copy-done.1), custom_call_target="tpu_custom_call" | custom-call | tf_op jit(solution)/shard_map/arrange_factors/pallas_call | solution.py:67
  2.9 3.9 %collective-permute-start.2 = (bf16[2,8,2,64,256]{4,3,2,1,0:T(8,128)(2,1)S(1)}, bf16[2,8,2,64,256]{4,3,2,1,0:T(8,128)(2,1)S(1)}, u32[]{:S(2)}, u32[]{:S(2)}) collective-permute-start(bf16[2,8,2,64,256]{4,3,2,1,0:T(8,128)(2,1)S(1)} %get-tuple-element.15.refs_1_), channel_id=1, source_target_pairs={{0,1},{1,2},{2,3},{3,0},{4,5},{5,6},{6,7},{7,4},{8,9},{9,10},{10,1... | collective-permute-start | bytes 3145736 | tf_op jit(solution)/shard_map/ppermute | solution.py:352
  6.8 3.2 %collective-permute-start = (bf16[8,2,64,256]{3,2,1,0:T(8,128)(2,1)}, bf16[8,2,64,256]{3,2,1,0:T(8,128)(2,1)S(1)}, u32[]{:S(2)}, u32[]{:S(2)}) collective-permute-start(bf16[8,2,64,256]{3,2,1,0:T(8,128)(2,1)} %get-tuple-element.14), channel_id=1, source_target_pairs={{0,3},{1,0},{2,1},{3,2},{4,7},{5,4},{6,5},{7,6},{8,11},{9,8},{10,9... | collective-permute-start | bytes 1572872 | tf_op jit(solution)/shard_map/ppermute | solution.py:353
  10.0 2.4 %pack_tiles.1 = (bf16[16,144,128]{2,1,0:T(8,128)(2,1)}, s32[16]{0:T(128)}) custom-call(s32[1]{0:T(128)} %bitcast.lead_ref, s32[2,16]{1,0:T(2,128)} %bitcast.19, s32[16]{0:T(128)} %live_hbm.1, s32[128]{0:T(128)} %owner_hbm.1, bf16[16,8,4096]{2,1,0:T(8,128)(2,1)} %amp_hbm.1), custom_call_target="tpu_custom_call" | custom-call | tf_op jit(solution)/shard_map/pack_tiles/pallas_call | solution.py:160
  12.5 13.8 %all-to-all-start = ((bf16[16,144,128]{2,1,0:T(8,128)(2,1)}), bf16[16,144,128]{2,1,0:T(8,128)(2,1)S(1)}, u32[]{:S(2)}, u32[]{:S(2)}) async-start(bf16[16,144,128]{2,1,0:T(8,128)(2,1)} %get-tuple-element.13), calls=%async_computation | async-start | bytes 1179648 | tf_op jit(solution)/shard_map/all_to_all | solution.py:361
  26.3 0.8 slice_bitcast_fusion.1
  27.1 1.9 %collective-permute-start.4 = (bf16[8,2,64,256]{3,2,1,0:T(8,128)(2,1)}, bf16[8,2,64,256]{3,2,1,0:T(8,128)(2,1)}, u32[]{:S(2)}, u32[]{:S(2)}) collective-permute-start(bf16[8,2,64,256]{3,2,1,0:T(8,128)(2,1)} %slice_bitcast_fusion.1), channel_id=1, source_target_pairs={{0,3},{1,0},{2,1},{3,2},{4,7},{5,4},{6,5},{7,6},{8,11},{9,8},{10,9... | collective-permute-start | bytes 1572872 | tf_op jit(solution)/shard_map/ppermute | solution.py:355
  29.1 0.0 collective-permute-done.piece_ref.refs_3_
  29.1 0.0 copy-start.2
  29.1 0.8 copy-done.2
  29.9 1.9 %relay.1 = bf16[8,2,64,256]{3,2,1,0:T(8,128)(2,1)} custom-call(bf16[8,2,64,256]{3,2,1,0:T(8,128)(2,1)} %copy-done.2), custom_call_target="tpu_custom_call" | custom-call | flops 1000000000 | bytes 8 | tf_op jit(solution)/shard_map/relay/pallas_call | solution.py:91
  31.7 0.0 copy-start.3
  31.8 2.1 %collective-permute-start.1 = (bf16[8,2,64,256]{3,2,1,0:T(8,128)(2,1)}, bf16[8,2,64,256]{3,2,1,0:T(8,128)(2,1)}, u32[]{:S(2)}, u32[]{:S(2)}) collective-permute-start(bf16[8,2,64,256]{3,2,1,0:T(8,128)(2,1)} %relay.1), channel_id=1, source_target_pairs={{0,3},{1,0},{2,1},{3,2},{4,7},{5,4},{6,5},{7,6},{8,11},{9,8},{10,9... | collective-permute-start | bytes 1572872 | tf_op jit(solution)/shard_map/ppermute | solution.py:354
  33.8 0.0 collective-permute-done.2.refs_2_
  33.8 0.8 slice_bitcast_fusion
  34.7 3.4 %collective-permute-start.3 = (bf16[8,2,64,256]{3,2,1,0:T(8,128)(2,1)}, bf16[8,2,64,256]{3,2,1,0:T(8,128)(2,1)}, u32[]{:S(2)}, u32[]{:S(2)}) collective-permute-start(bf16[8,2,64,256]{3,2,1,0:T(8,128)(2,1)} %slice_bitcast_fusion), channel_id=1, source_target_pairs={{0,1},{1,2},{2,3},{3,0},{4,5},{5,6},{6,7},{7,4},{8,9},{9,10},{10,1... | collective-permute-start | bytes 1572872 | tf_op jit(solution)/shard_map/ppermute | solution.py:356
  38.0 4.6 %collective-permute-done.4.refs_4_ = bf16[8,2,64,256]{3,2,1,0:T(8,128)(2,1)} collective-permute-done((bf16[8,2,64,256]{3,2,1,0:T(8,128)(2,1)}, bf16[8,2,64,256]{3,2,1,0:T(8,128)(2,1)}, u32[]{:S(2)}, u32[]{:S(2)}) %collective-permute-start.4) | collective-permute-done | bytes 524320 | tf_op jit(solution)/shard_map/ppermute | solution.py:355
  42.6 2.3 %all-to-all-done.refs_0_ = bf16[16,144,128]{2,1,0:T(8,128)(2,1)S(1)} async-done(((bf16[16,144,128]{2,1,0:T(8,128)(2,1)}), bf16[16,144,128]{2,1,0:T(8,128)(2,1)S(1)}, u32[]{:S(2)}, u32[]{:S(2)}) %all-to-all-start) | async-done | bytes 589856 | tf_op jit(solution)/shard_map/all_to_all | solution.py:361
  44.9 0.0 copy-done.3
  44.9 8.3 %ladder_terms.2.refs_3_ = f32[32,64,128]{2,1,0:T(8,128)S(1)} custom-call(bf16[16,144,128]{2,1,0:T(8,128)(2,1)S(1)} %all-to-all-done.refs_0_, bf16[2,8,2,64,256]{4,3,2,1,0:T(8,128)(2,1)S(1)} %get-tuple-element.15.refs_1_, bf16[2,8,2,64,256]{4,3,2,1,0:T(8,128)(2,1)S(1)} %collective-permute-done.2.refs_2_, bf16[8,2,64,256]{3,2,1,0:T(8,128)(2,1)S(1)} %copy-done.3, ...), custom_call_target="tpu_custom_call" | custom-call | flops 10000000 | bytes 3145728 | tf_op jit(solution)/shard_map/ladder_terms/pallas_call | solution.py:287
  53.2 0.0 copy-start.7
  53.2 0.7 collective-permute-done.1.refs_1_
  53.9 0.0 collective-permute-done.3.refs_2_
  53.9 4.5 %ladder_terms.3 = bf16[32,64,128]{2,1,0:T(8,128)(2,1)} custom-call(bf16[16,144,128]{2,1,0:T(8,128)(2,1)S(1)} %all-to-all-done.refs_0_, bf16[8,2,64,256]{3,2,1,0:T(8,128)(2,1)} %collective-permute-done.1.refs_1_, bf16[8,2,64,256]{3,2,1,0:T(8,128)(2,1)} %collective-permute-done.3.refs_2_, f32[32,64,128]{2,1,0:T(8,128)S(1)} %ladder_terms.2.refs_3_), custom_call_target="tpu_custom_call" | custom-call | flops 10000000 | bytes 1048576 | tf_op jit(solution)/shard_map/ladder_terms/pallas_call | solution.py:287
  58.4 0.0 copy-done.7
  58.4 0.0 copy-start.5
  58.5 8.1 %all-to-all-start.1 = ((bf16[32,64,128]{2,1,0:T(8,128)(2,1)}), bf16[32,64,128]{2,1,0:T(8,128)(2,1)S(1)}, u32[]{:S(2)}, u32[]{:S(2)}) async-start(bf16[32,64,128]{2,1,0:T(8,128)(2,1)} %ladder_terms.3), calls=%async_computation.1 | async-start | bytes 1048576 | tf_op jit(solution)/shard_map/all_to_all | solution.py:366
  66.5 0.0 copy-done
  66.5 0.2 convolution_bitcast_fusion
  66.7 0.0 copy-start.6
  66.7 0.1 copy.8
  66.8 0.6 copy-done.6
  67.4 0.1 iota_compare_fusion.1
  67.5 0.1 broadcast_and_fusion
  67.6 0.2 convert_element_type.15
  67.8 0.0 copy-done.5
  67.8 0.3 fusion.cycle_ref
  68.1 0.0 copy-start.4
  68.1 15.8 %all-to-all-done.1.returned_ref = bf16[32,64,128]{2,1,0:T(8,128)(2,1)S(1)} async-done(((bf16[32,64,128]{2,1,0:T(8,128)(2,1)}), bf16[32,64,128]{2,1,0:T(8,128)(2,1)S(1)}, u32[]{:S(2)}, u32[]{:S(2)}) %all-to-all-start.1) | async-done | bytes 524320 | tf_op jit(solution)/shard_map/all_to_all | solution.py:366
  83.9 0.0 copy-done.4
  83.9 1.5 %finish_tiles.1 = bf16[16,2,4096]{2,1,0:T(2,128)(2,1)} custom-call(s32[16]{0:T(128)S(1)} %copy-done.4, bf16[32,64,128]{2,1,0:T(8,128)(2,1)S(1)} %all-to-all-done.1.returned_ref, f32[32,4096]{1,0:T(8,128)S(1)} %fusion.cycle_ref), custom_call_target="tpu_custom_call" | custom-call | tf_op jit(solution)/shard_map/finish_tiles/pallas_call | solution.py:315
  (3 shorter events, 0.0 us)
Async XLA Ops:
  0.0 66.5 %copy-start = (bf16[64,8,8]{0,2,1:T(8,128)(2,1)S(1)}, bf16[64,8,8]{0,2,1:T(8,128)(2,1)}, u32[]{:S(2)}) copy-start(bf16[64,8,8]{0,2,1:T(8,128)(2,1)} %param.10) | copy-start | bytes 24580
  0.0 1.2 %copy-start.1 = (bf16[8,2,8,4096]{3,2,1,0:T(8,128)(2,1)S(1)}, bf16[8,2,8,4096]{3,2,1,0:T(8,128)(2,1)}, u32[]{:S(2)}) copy-start(bf16[8,2,8,4096]{3,2,1,0:T(8,128)(2,1)} %factor_ref.1) | copy-start | bytes 3145732
  2.9 30.9 %collective-permute-start.2 = (bf16[2,8,2,64,256]{4,3,2,1,0:T(8,128)(2,1)S(1)}, bf16[2,8,2,64,256]{4,3,2,1,0:T(8,128)(2,1)S(1)}, u32[]{:S(2)}, u32[]{:S(2)}) collective-permute-start(bf16[2,8,2,64,256]{4,3,2,1,0:T(8,128)(2,1)S(1)} %get-tuple-element.15.refs_1_), channel_id=1, source_target_pairs={{0,1},{1,2},{2,3},{3,0},{4,5},{5,6},{6,7},{7,4},{8,9},{9,10},{10,1... | collective-permute-start | bytes 3145736 | tf_op jit(solution)/shard_map/ppermute | solution.py:352
  6.8 22.2 %collective-permute-start = (bf16[8,2,64,256]{3,2,1,0:T(8,128)(2,1)}, bf16[8,2,64,256]{3,2,1,0:T(8,128)(2,1)S(1)}, u32[]{:S(2)}, u32[]{:S(2)}) collective-permute-start(bf16[8,2,64,256]{3,2,1,0:T(8,128)(2,1)} %get-tuple-element.14), channel_id=1, source_target_pairs={{0,3},{1,0},{2,1},{3,2},{4,7},{5,4},{6,5},{7,6},{8,11},{9,8},{10,9... | collective-permute-start | bytes 1572872 | tf_op jit(solution)/shard_map/ppermute | solution.py:353
  12.5 32.5 %all-to-all-start = ((bf16[16,144,128]{2,1,0:T(8,128)(2,1)}), bf16[16,144,128]{2,1,0:T(8,128)(2,1)S(1)}, u32[]{:S(2)}, u32[]{:S(2)}) async-start(bf16[16,144,128]{2,1,0:T(8,128)(2,1)} %get-tuple-element.13), calls=%async_computation | async-start | bytes 1179648 | tf_op jit(solution)/shard_map/all_to_all | solution.py:361
  27.1 15.5 %collective-permute-start.4 = (bf16[8,2,64,256]{3,2,1,0:T(8,128)(2,1)}, bf16[8,2,64,256]{3,2,1,0:T(8,128)(2,1)}, u32[]{:S(2)}, u32[]{:S(2)}) collective-permute-start(bf16[8,2,64,256]{3,2,1,0:T(8,128)(2,1)} %slice_bitcast_fusion.1), channel_id=1, source_target_pairs={{0,3},{1,0},{2,1},{3,2},{4,7},{5,4},{6,5},{7,6},{8,11},{9,8},{10,9... | collective-permute-start | bytes 1572872 | tf_op jit(solution)/shard_map/ppermute | solution.py:355
  29.1 0.8 copy-start.2
  31.7 13.2 %copy-start.3 = (bf16[8,2,64,256]{3,2,1,0:T(8,128)(2,1)S(1)}, bf16[8,2,64,256]{3,2,1,0:T(8,128)(2,1)}, u32[]{:S(2)}) copy-start(bf16[8,2,64,256]{3,2,1,0:T(8,128)(2,1)} %copy-done.2) | copy-start | bytes 1572868
  31.8 22.1 %collective-permute-start.1 = (bf16[8,2,64,256]{3,2,1,0:T(8,128)(2,1)}, bf16[8,2,64,256]{3,2,1,0:T(8,128)(2,1)}, u32[]{:S(2)}, u32[]{:S(2)}) collective-permute-start(bf16[8,2,64,256]{3,2,1,0:T(8,128)(2,1)} %relay.1), channel_id=1, source_target_pairs={{0,3},{1,0},{2,1},{3,2},{4,7},{5,4},{6,5},{7,6},{8,11},{9,8},{10,9... | collective-permute-start | bytes 1572872 | tf_op jit(solution)/shard_map/ppermute | solution.py:354
  34.7 19.2 %collective-permute-start.3 = (bf16[8,2,64,256]{3,2,1,0:T(8,128)(2,1)}, bf16[8,2,64,256]{3,2,1,0:T(8,128)(2,1)}, u32[]{:S(2)}, u32[]{:S(2)}) collective-permute-start(bf16[8,2,64,256]{3,2,1,0:T(8,128)(2,1)} %slice_bitcast_fusion), channel_id=1, source_target_pairs={{0,1},{1,2},{2,3},{3,0},{4,5},{5,6},{6,7},{7,4},{8,9},{9,10},{10,1... | collective-permute-start | bytes 1572872 | tf_op jit(solution)/shard_map/ppermute | solution.py:356
  53.2 5.2 %copy-start.7 = (s32[16,2]{0,1:T(2,128)S(1)}, s32[16,2]{0,1:T(2,128)}, u32[]{:S(2)}) copy-start(s32[16,2]{0,1:T(2,128)} %param.7) | copy-start | bytes 388
  58.4 9.4 %copy-start.5 = (bf16[16,8,4096]{2,1,0:T(8,128)(2,1)S(1)}, bf16[16,8,4096]{2,1,0:T(8,128)(2,1)}, u32[]{:S(2)}) copy-start(bf16[16,8,4096]{2,1,0:T(8,128)(2,1)} %amp_hbm.1) | copy-start | bytes 3145732
  58.5 25.4 %all-to-all-start.1 = ((bf16[32,64,128]{2,1,0:T(8,128)(2,1)}), bf16[32,64,128]{2,1,0:T(8,128)(2,1)S(1)}, u32[]{:S(2)}, u32[]{:S(2)}) async-start(bf16[32,64,128]{2,1,0:T(8,128)(2,1)} %ladder_terms.3), calls=%async_computation.1 | async-start | bytes 1048576 | tf_op jit(solution)/shard_map/all_to_all | solution.py:366
  66.7 0.7 copy-start.6
  68.1 15.8 %copy-start.4 = (s32[16]{0:T(128)S(1)}, s32[16]{0:T(128)}, u32[]{:S(2)}) copy-start(s32[16]{0:T(128)} %get-tuple-element.12.slot_ref) | copy-start | bytes 196

commit v5 on v2

--- a/solution.py
+++ b/solution.py
@@ -11,8 +11,8 @@
 LANES = 128
 LABEL_ROWS = 16
 FAR_UP = 9
-CHUNK = 4
-UNROLL = 16
+CHUNK = 8
+UNROLL = 32
 PIECE = 16
 OUT_SLOTS = 8
 PACK_VMEM = 57 * 1024 * 1024
@@ -58,7 +58,7 @@
                         out_ref[2 * v + half, 1, :, lanes] = woven[spot].astype(jnp.bfloat16)
         return carry
 
-    lax.fori_loop(0, factor_ref.shape[0], one, 0)
+    lax.fori_loop(0, factor_ref.shape[0], one, 0, unroll=4)
 
 
 def arrange_factors(factors):
@@ -278,53 +278,88 @@
 
 
 def finish_kernel(slot_ref, returned_ref, cycle_ref, out_ref, scratch):
-    for k in range(out_ref.shape[0]):
-        spot = k % 2
-        block = returned_ref[slot_ref[k]].astype(jnp.float32)
-        for p in range(2):
-            scratch[spot, pl.ds(p, 32, stride=2), :] = block[p * 32 : (p + 1) * 32]
+    for g in range(out_ref.shape[0] // 4):
+        spot = g % 2
+        for j in range(4):
+            block = returned_ref[slot_ref[4 * g + j]].astype(jnp.float32)
+            for p in range(2):
+                scratch[spot, pl.ds(2 * j + p, 32, stride=8), :] = block[p * 32 : (p + 1) * 32]
         for t in range(32):
             lanes = slice(t * LANES, (t + 1) * LANES)
-            total = scratch[spot, 2 * t : 2 * t + 2, :] + cycle_ref[k, :, lanes]
-            out_ref[k, :, lanes] = total.astype(jnp.bfloat16)
+            total = scratch[spot, 8 * t : 8 * t + 8, :] + cycle_ref[8 * g : 8 * g + 8, lanes]
+            for j in range(4):
+                out_ref[4 * g + j, :, lanes] = total[2 * j : 2 * j + 2].astype(jnp.bfloat16)
 
 
 def finish(slot, returned, cycle):
     vmem = pl.BlockSpec(memory_space=pltpu.VMEM)
     return pl.pallas_call(
         finish_kernel,
-        out_shape=jax.ShapeDtypeStruct(cycle.shape, jnp.bfloat16),
+        out_shape=jax.ShapeDtypeStruct((cycle.shape[0] // 2, 2, cycle.shape[1]), jnp.bfloat16),
         in_specs=[pl.BlockSpec(memory_space=pltpu.SMEM), vmem, vmem],
         out_specs=vmem,
-        scratch_shapes=[pltpu.VMEM((2, VB, LANES), jnp.float32)],
+        scratch_shapes=[pltpu.VMEM((2, 256, LANES), jnp.float32)],
         compiler_params=pltpu.CompilerParams(vmem_limit_bytes=SMALL_VMEM),
         name="finish_tiles",
     )(slot, returned, cycle)
 
 
-def cycle_terms(lead, share, amplitudes, tile_blocks, live_rows, cycle_coupling):
+def cycle_kernel(
+    lead_ref, blocks_hbm, live_hbm, coupling_ref, amp_ref, after_ref, out_ref, held, mixing, blocks_ref, live_ref, sems
+):
+    tables = [
+        pltpu.make_async_copy(blocks_hbm, blocks_ref, sems.at[0]),
+        pltpu.make_async_copy(live_hbm, live_ref, sems.at[1]),
+    ]
+    for copy in tables:
+        copy.start()
+    tiles, rows, cells = amp_ref.shape
+    lead = lead_ref[0]
+    held[...] = jnp.zeros(held.shape, held.dtype)
+    lane = lax.broadcasted_iota(jnp.int32, (rows, rows), 1)
+    for copy in tables:
+        copy.wait()
+    for k in range(tiles):
+        block = coupling_ref[blocks_ref[0, k]].astype(jnp.float32)
+        held[k, :, 0:rows] = jnp.where(lane < live_ref[k], block, 0.0)
+        for p in range(2):
+            row = held[k, pl.ds(lead + p, 1), :]
+            mixing[2 * k + p : 2 * k + p + 1, :] = pltpu.roll(row, rows * k, 1) if k else row
+    mix = mixing[...].astype(jnp.bfloat16)
+    for begin in range(0, cells, 512):
+        lanes = slice(begin, begin + 512)
+        out_ref[:, lanes] = jnp.dot(
+            mix, amp_ref[:, :, lanes].reshape(tiles * rows, 512), preferred_element_type=jnp.float32
+        )
+
+
+def cycle_terms(lead, tile_blocks, live_rows, cycle_coupling, amplitudes, after):
     tiles, rows, cells = amplitudes.shape
-    chosen = (tile_blocks[:, 0:1] == jnp.arange(cycle_coupling.shape[0])[None, :]).astype(jnp.bfloat16)
-    mine = lax.dynamic_slice_in_dim(cycle_coupling, lead, share, 1)
-    coupling = jnp.einsum("kn,npq->kpq", chosen, mine, preferred_element_type=jnp.float32)
-    live = jnp.arange(rows)[None, :] < live_rows[:, None]
-    same = jnp.eye(tiles, dtype=bool)
-    mixing = jnp.where(
-        same[:, None, :, None] & live[:, None, None, :], coupling[:, :, None, :], 0.0
-    ).astype(jnp.bfloat16)
-    cycle = jnp.dot(
-        mixing.reshape(tiles * share, tiles * rows),
-        amplitudes.reshape(tiles * rows, cells),
-        preferred_element_type=jnp.float32,
-    )
-    return cycle.reshape(tiles, share, cells)
+    smem, vmem = pl.BlockSpec(memory_space=pltpu.SMEM), pl.BlockSpec(memory_space=pltpu.VMEM)
+    hbm = pl.BlockSpec(memory_space=pltpu.HBM)
+    return pl.pallas_call(
+        cycle_kernel,
+        out_shape=jax.ShapeDtypeStruct((2 * tiles, cells), jnp.float32),
+        in_specs=[smem, hbm, hbm, vmem, vmem, pl.BlockSpec(memory_space=pl.ANY)],
+        out_specs=vmem,
+        scratch_shapes=[
+            pltpu.VMEM((tiles, rows, LANES), jnp.float32),
+            pltpu.VMEM((2 * tiles, LANES), jnp.float32),
+            pltpu.SMEM(tile_blocks.shape, jnp.int32),
+            pltpu.SMEM(live_rows.shape, jnp.int32),
+            pltpu.SemaphoreType.DMA((2,)),
+        ],
+        compiler_params=pltpu.CompilerParams(vmem_limit_bytes=SMALL_VMEM),
+        name="cycle_terms",
+    )(lead, tile_blocks, live_rows, cycle_coupling, amplitudes, after)
 
 
 def local(amplitudes, tile_blocks, live_rows, ladder_factors, cycle_coupling, block_owner):
     peers = lax.axis_size("tile")
     reps = lax.axis_size("rep")
     share = amplitudes.shape[1] // reps
-    lead = lax.axis_index("rep") * share
+    lead = (lax.axis_index("rep") * share).astype(jnp.int32).reshape(1)
+    blocks = tile_blocks.T
     up = [(i, (i + 1) % reps) for i in range(reps)]
     down = [(i, (i - 1) % reps) for i in range(reps)]
 
@@ -334,13 +369,11 @@
     far_first = lax.ppermute(below[:FAR_UP], "rep", up)
     far_second = lax.ppermute(above[FAR_UP:], "rep", down)
 
-    packed, slot = pack(
-        lead.astype(jnp.int32).reshape(1), tile_blocks.T, live_rows, block_owner, amplitudes, peers
-    )
+    packed, slot = pack(lead, blocks, live_rows, block_owner, amplitudes, peers)
     buffer = lax.all_to_all(packed, "tile", split_axis=0, concat_axis=0, tiled=True)
-    cycle = cycle_terms(lead, share, amplitudes, tile_blocks, live_rows, cycle_coupling)
     earlier = ladder_terms(buffer, (own, below, above), ((0, 0), (1, 0), (2, 0)))
     terms = ladder_terms(buffer, (far_first, far_second), ((0, 0), (0, FAR_UP)), earlier)
+    cycle = cycle_terms(lead, blocks, live_rows, cycle_coupling, amplitudes, terms)
     returned = lax.all_to_all(terms, "tile", split_axis=0, concat_axis=0, tiled=True)
     return finish(slot, returned, cycle)
 

time: 82.1 us -> 81.5 us (level)
  waiting for transfers between devices: 20.8 us -> 21.8 us
  matrix products: 0.98 us -> 0 us
  local copies, waits for them, and re-layouts: 5.53 us -> 4.62 us
    all_to_all x1, waiting for transfers between devices: 14.6 us -> 15.6 us  [local(): lax.all_to_all(terms, 'tile', split_axis=0, concat_axis=0, tiled=True)]
    pallas_call x1 -> x2, Pallas kernels: 1.56 us -> 2.48 us  [the longest x1 1.49 us: finish(): pl.pallas_call(finish_kernel, out_shape=jax.ShapeDtypeStruct((cycle.shape...]
    unnamed x12 -> x13, local copies, waits for them, and re-layouts: 2.39 us -> 1.9 us
  transfers between devices with their start and end apart: 6 -> 6, of which waited for: 2 -> 2; matrix products, arithmetic and copies ran while one was open for 5% -> 4% of each run, Pallas kernels for 14% -> 15%
where the time goes in v5:
time: 81.5 us; the launch traced here: 80.8 us
  starting transfers between devices  35.6 us (44%)
  waiting for transfers between devices  21.8 us (27%)
  Pallas kernels  18.6 us (23%)
  local copies, waits for them, and re-layouts  4.62 us (6%)
    all_to_all x1, waiting for transfers between devices, local(): lax.all_to_all(terms, 'tile', split_axis=0, concat_axis=0, tiled=True)  15.6 us
    all_to_all x1, starting transfers between devices, local(): lax.all_to_all(packed, 'tile', split_axis=0, concat_axis=0, tiled=True)  13.8 us
    pallas_call x2, Pallas kernels, ladder_terms(): pl.pallas_call(lambda *refs: ladder_kernel(places, more, *refs), out_shap...  12.9 us
    all_to_all x1, waiting for transfers between devices, local(): lax.all_to_all(packed, 'tile', split_axis=0, concat_axis=0, tiled=True)  6.16 us
    ppermute x1, starting transfers between devices, local(): far_first = lax.ppermute(below[:FAR_UP], 'rep', up)  5.45 us
    all_to_all x1, starting transfers between devices, local(): lax.all_to_all(terms, 'tile', split_axis=0, concat_axis=0, tiled=True)  4.98 us
    ppermute x1, starting transfers between devices, local(): far_second = lax.ppermute(above[FAR_UP:], 'rep', down)  4.27 us
    ppermute x1, starting transfers between devices, local(): below = lax.ppermute(own, 'rep', up)  3.95 us
  transfers between devices with their start and end apart: 6, of which 2 were waited for; matrix products, arithmetic and copies ran while one was open for 4% of the time, Pallas kernels for 15%

profile of v5, /device:TPU:1, one launch (start us, length us, event | category | flops | bytes accessed | tf_op | source)
XLA Modules:
  0.0 80.8 jit_solution(13938773706412388207)
XLA Ops:
  0.0 0.0 copy-start.1
  0.0 1.2 %copy-done.1 = bf16[8,2,8,4096]{3,2,1,0:T(8,128)(2,1)S(1)} copy-done((bf16[8,2,8,4096]{3,2,1,0:T(8,128)(2,1)S(1)}, bf16[8,2,8,4096]{3,2,1,0:T(8,128)(2,1)}, u32[]{:S(2)}) %copy-start.1) | copy-done | bytes 1048600
  1.2 0.8 %arrange_factors.1.refs_1_ = bf16[16,2,64,256]{3,2,1,0:T(8,128)(2,1)S(1)} custom-call(bf16[8,2,8,4096]{3,2,1,0:T(8,128)(2,1)S(1)} %copy-done.1), custom_call_target="tpu_custom_call" | custom-call | tf_op jit(solution)/shard_map/arrange_factors/pallas_call | solution.py:66
  2.1 3.9 %collective-permute-start = (bf16[16,2,64,256]{3,2,1,0:T(8,128)(2,1)S(1)}, bf16[16,2,64,256]{3,2,1,0:T(8,128)(2,1)S(1)}, u32[]{:S(2)}, u32[]{:S(2)}) collective-permute-start(bf16[16,2,64,256]{3,2,1,0:T(8,128)(2,1)S(1)} %arrange_factors.1.refs_1_), channel_id=1, source_target_pairs={{0,1},{1,2},{2,3},{3,0},{4,5},{5,6},{6,7},{7,4},{8,9},{9,10},{10,1... | collective-permute-start | bytes 3145736 | tf_op jit(solution)/shard_map/ppermute | solution.py:367
  6.0 3.2 %collective-permute-start.2 = (bf16[16,2,64,256]{3,2,1,0:T(8,128)(2,1)S(1)}, bf16[16,2,64,256]{3,2,1,0:T(8,128)(2,1)}, u32[]{:S(2)}, u32[]{:S(2)}) collective-permute-start(bf16[16,2,64,256]{3,2,1,0:T(8,128)(2,1)S(1)} %arrange_factors.1.refs_1_), channel_id=1, source_target_pairs={{0,3},{1,0},{2,1},{3,2},{4,7},{5,4},{6,5},{7,6},{8,11},{9,8},{10,9... | collective-permute-start | bytes 3145736 | tf_op jit(solution)/shard_map/ppermute | solution.py:368
  9.2 2.4 %pack_tiles.1 = (bf16[16,144,128]{2,1,0:T(8,128)(2,1)}, s32[16]{0:T(128)}) custom-call(s32[1]{0:T(128)} %bitcast.lead_ref, s32[2,16]{1,0:T(2,128)} %bitcast.2, s32[16]{0:T(128)} %live_hbm.3, s32[128]{0:T(128)} %owner_hbm.1, bf16[16,8,4096]{2,1,0:T(8,128)(2,1)} %amp_ref.1), custom_call_target="tpu_custom_call" | custom-call | tf_op jit(solution)/shard_map/pack_tiles/pallas_call | solution.py:138
  11.7 13.8 %all-to-all-start = ((bf16[16,144,128]{2,1,0:T(8,128)(2,1)}), bf16[16,144,128]{2,1,0:T(8,128)(2,1)S(1)}, u32[]{:S(2)}, u32[]{:S(2)}) async-start(bf16[16,144,128]{2,1,0:T(8,128)(2,1)} %get-tuple-element.8), calls=%async_computation | async-start | bytes 1179648 | tf_op jit(solution)/shard_map/all_to_all | solution.py:373
  25.5 0.0 collective-permute-done.refs_2_
  25.5 0.9 %slice.8 = bf16[9,2,64,256]{3,2,1,0:T(8,128)(2,1)} slice(bf16[16,2,64,256]{3,2,1,0:T(8,128)(2,1)S(1)} %collective-permute-done.refs_2_), slice={[0:9], [0:2], [0:64], [0:256]} | slice | bytes 1179648 | tf_op jit(solution)/shard_map/slice | solution.py:369
  26.4 5.4 %collective-permute-start.1 = (bf16[9,2,64,256]{3,2,1,0:T(8,128)(2,1)}, bf16[9,2,64,256]{3,2,1,0:T(8,128)(2,1)S(1)}, u32[]{:S(2)}, u32[]{:S(2)}) collective-permute-start(bf16[9,2,64,256]{3,2,1,0:T(8,128)(2,1)} %slice.8), channel_id=1, source_target_pairs={{0,1},{1,2},{2,3},{3,0},{4,5},{5,6},{6,7},{7,4},{8,9},{9,10},{10,1... | collective-permute-start | bytes 1769480 | tf_op jit(solution)/shard_map/ppermute | solution.py:369
  31.8 0.0 collective-permute-done.2.refs_3_
  31.8 1.8 %slice.9 = bf16[7,2,64,256]{3,2,1,0:T(8,128)(2,1)} slice(bf16[16,2,64,256]{3,2,1,0:T(8,128)(2,1)} %collective-permute-done.2.refs_3_), slice={[9:16], [0:2], [0:64], [0:256]} | slice | bytes 917504 | tf_op jit(solution)/shard_map/slice | solution.py:370
  33.7 4.3 %collective-permute-start.3 = (bf16[7,2,64,256]{3,2,1,0:T(8,128)(2,1)}, bf16[7,2,64,256]{3,2,1,0:T(8,128)(2,1)}, u32[]{:S(2)}, u32[]{:S(2)}) collective-permute-start(bf16[7,2,64,256]{3,2,1,0:T(8,128)(2,1)} %slice.9), channel_id=1, source_target_pairs={{0,3},{1,0},{2,1},{3,2},{4,7},{5,4},{6,5},{7,6},{8,11},{9,8},{10,9... | collective-permute-start | bytes 1376264 | tf_op jit(solution)/shard_map/ppermute | solution.py:370
  37.9 6.2 %all-to-all-done.refs_0_ = bf16[16,144,128]{2,1,0:T(8,128)(2,1)S(1)} async-done(((bf16[16,144,128]{2,1,0:T(8,128)(2,1)}), bf16[16,144,128]{2,1,0:T(8,128)(2,1)S(1)}, u32[]{:S(2)}, u32[]{:S(2)}) %all-to-all-start) | async-done | bytes 589856 | tf_op jit(solution)/shard_map/all_to_all | solution.py:373
  44.1 8.4 %ladder_terms.2.refs_3_ = f32[32,64,128]{2,1,0:T(8,128)S(1)} custom-call(bf16[16,144,128]{2,1,0:T(8,128)(2,1)S(1)} %all-to-all-done.refs_0_, bf16[16,2,64,256]{3,2,1,0:T(8,128)(2,1)S(1)} %arrange_factors.1.refs_1_, bf16[16,2,64,256]{3,2,1,0:T(8,128)(2,1)S(1)} %collective-permute-done.refs_2_, bf16[16,2,64,256]{3,2,1,0:T(8,128)(2,1)} %collective-permute-done.2.refs_3_), custom_call_target="tpu_custom_call" | custom-call | flops 10000000 | bytes 3145728 | tf_op jit(solution)/shard_map/ladder_terms/pallas_call | solution.py:268
  52.5 0.0 collective-permute-done.3.refs_2_
  52.5 0.0 collective-permute-done.1.refs_1_
  52.5 0.0 copy-start.5
  52.5 4.5 %ladder_terms.3.after_ref = bf16[32,64,128]{2,1,0:T(8,128)(2,1)} custom-call(bf16[16,144,128]{2,1,0:T(8,128)(2,1)S(1)} %all-to-all-done.refs_0_, bf16[9,2,64,256]{3,2,1,0:T(8,128)(2,1)S(1)} %collective-permute-done.1.refs_1_, bf16[7,2,64,256]{3,2,1,0:T(8,128)(2,1)} %collective-permute-done.3.refs_2_, f32[32,64,128]{2,1,0:T(8,128)S(1)} %ladder_terms.2.refs_3_), custom_call_target="tpu_custom_call" | custom-call | flops 10000000 | bytes 1048576 | tf_op jit(solution)/shard_map/ladder_terms/pallas_call | solution.py:268
  57.0 0.0 copy-start
  57.0 5.0 %all-to-all-start.1 = ((bf16[32,64,128]{2,1,0:T(8,128)(2,1)}), bf16[32,64,128]{2,1,0:T(8,128)(2,1)S(1)}, u32[]{:S(2)}, u32[]{:S(2)}) async-start(bf16[32,64,128]{2,1,0:T(8,128)(2,1)} %ladder_terms.3.after_ref), calls=%async_computation.1 | async-start | bytes 1048576 | tf_op jit(solution)/shard_map/all_to_all | solution.py:377
  62.0 0.0 copy-done.5
  62.0 0.0 copy-start.2
  62.0 0.0 copy-start.3
  62.1 0.1 copy.7.coupling_ref
  62.2 0.0 copy-done
  62.2 0.5 copy-done.2
  62.7 0.0 copy-done.3
  62.7 1.0 %cycle_terms.1.cycle_ref = f32[32,4096]{1,0:T(8,128)S(1)} custom-call(s32[1]{0:T(128)} %bitcast.lead_ref, s32[2,16]{1,0:T(2,128)S(1)} %bitcast.3, s32[16]{0:T(128)S(1)} %copy-done.3, bf16[64,8,8]{2,1,0:T(8,128)(2,1)S(1)} %copy.7.coupling_ref, bf16[16,8,4096]{2,1,0:T(8,128)(2,1)S(1)} %copy-done, bf16[32,64,128]{2,1,0:T(8,128)(2,1)} %ladder_terms.3.after_ref), custom_call_target="tpu_custom_call" | custom-call | tf_op jit(solution)/shard_map/cycle_terms/pallas_call | solution.py:340
  63.7 0.0 copy-start.4
  63.7 15.6 %all-to-all-done.1.returned_ref = bf16[32,64,128]{2,1,0:T(8,128)(2,1)S(1)} async-done(((bf16[32,64,128]{2,1,0:T(8,128)(2,1)}), bf16[32,64,128]{2,1,0:T(8,128)(2,1)S(1)}, u32[]{:S(2)}, u32[]{:S(2)}) %all-to-all-start.1) | async-done | bytes 524320 | tf_op jit(solution)/shard_map/all_to_all | solution.py:377
  79.3 0.0 copy-done.4
  79.3 1.5 %finish_tiles.1 = bf16[16,2,4096]{2,1,0:T(2,128)(2,1)} custom-call(s32[16]{0:T(128)S(1)} %copy-done.4, bf16[32,64,128]{2,1,0:T(8,128)(2,1)S(1)} %all-to-all-done.1.returned_ref, f32[32,4096]{1,0:T(8,128)S(1)} %cycle_terms.1.cycle_ref), custom_call_target="tpu_custom_call" | custom-call | tf_op jit(solution)/shard_map/finish_tiles/pallas_call | solution.py:296
Async XLA Ops:
  0.0 1.2 %copy-start.1 = (bf16[8,2,8,4096]{3,2,1,0:T(8,128)(2,1)S(1)}, bf16[8,2,8,4096]{3,2,1,0:T(8,128)(2,1)}, u32[]{:S(2)}) copy-start(bf16[8,2,8,4096]{3,2,1,0:T(8,128)(2,1)} %factor_ref.1) | copy-start | bytes 3145732
  2.1 23.4 %collective-permute-start = (bf16[16,2,64,256]{3,2,1,0:T(8,128)(2,1)S(1)}, bf16[16,2,64,256]{3,2,1,0:T(8,128)(2,1)S(1)}, u32[]{:S(2)}, u32[]{:S(2)}) collective-permute-start(bf16[16,2,64,256]{3,2,1,0:T(8,128)(2,1)S(1)} %arrange_factors.1.refs_1_), channel_id=1, source_target_pairs={{0,1},{1,2},{2,3},{3,0},{4,5},{5,6},{6,7},{7,4},{8,9},{9,10},{10,1... | collective-permute-start | bytes 3145736 | tf_op jit(solution)/shard_map/ppermute | solution.py:367
  6.0 25.8 %collective-permute-start.2 = (bf16[16,2,64,256]{3,2,1,0:T(8,128)(2,1)S(1)}, bf16[16,2,64,256]{3,2,1,0:T(8,128)(2,1)}, u32[]{:S(2)}, u32[]{:S(2)}) collective-permute-start(bf16[16,2,64,256]{3,2,1,0:T(8,128)(2,1)S(1)} %arrange_factors.1.refs_1_), channel_id=1, source_target_pairs={{0,3},{1,0},{2,1},{3,2},{4,7},{5,4},{6,5},{7,6},{8,11},{9,8},{10,9... | collective-permute-start | bytes 3145736 | tf_op jit(solution)/shard_map/ppermute | solution.py:368
  11.7 32.5 %all-to-all-start = ((bf16[16,144,128]{2,1,0:T(8,128)(2,1)}), bf16[16,144,128]{2,1,0:T(8,128)(2,1)S(1)}, u32[]{:S(2)}, u32[]{:S(2)}) async-start(bf16[16,144,128]{2,1,0:T(8,128)(2,1)} %get-tuple-element.8), calls=%async_computation | async-start | bytes 1179648 | tf_op jit(solution)/shard_map/all_to_all | solution.py:373
  26.4 26.2 %collective-permute-start.1 = (bf16[9,2,64,256]{3,2,1,0:T(8,128)(2,1)}, bf16[9,2,64,256]{3,2,1,0:T(8,128)(2,1)S(1)}, u32[]{:S(2)}, u32[]{:S(2)}) collective-permute-start(bf16[9,2,64,256]{3,2,1,0:T(8,128)(2,1)} %slice.8), channel_id=1, source_target_pairs={{0,1},{1,2},{2,3},{3,0},{4,5},{5,6},{6,7},{7,4},{8,9},{9,10},{10,1... | collective-permute-start | bytes 1769480 | tf_op jit(solution)/shard_map/ppermute | solution.py:369
  33.7 18.8 %collective-permute-start.3 = (bf16[7,2,64,256]{3,2,1,0:T(8,128)(2,1)}, bf16[7,2,64,256]{3,2,1,0:T(8,128)(2,1)}, u32[]{:S(2)}, u32[]{:S(2)}) collective-permute-start(bf16[7,2,64,256]{3,2,1,0:T(8,128)(2,1)} %slice.9), channel_id=1, source_target_pairs={{0,3},{1,0},{2,1},{3,2},{4,7},{5,4},{6,5},{7,6},{8,11},{9,8},{10,9... | collective-permute-start | bytes 1376264 | tf_op jit(solution)/shard_map/ppermute | solution.py:370
  52.5 9.5 %copy-start.5 = (bf16[64,8,8]{0,2,1:T(8,128)(2,1)S(1)}, bf16[64,8,8]{0,2,1:T(8,128)(2,1)}, u32[]{:S(2)}) copy-start(bf16[64,8,8]{0,2,1:T(8,128)(2,1)} %param.10) | copy-start | bytes 24580
  57.0 5.2 %copy-start = (bf16[16,8,4096]{2,1,0:T(8,128)(2,1)S(1)}, bf16[16,8,4096]{2,1,0:T(8,128)(2,1)}, u32[]{:S(2)}) copy-start(bf16[16,8,4096]{2,1,0:T(8,128)(2,1)} %amp_ref.1) | copy-start | bytes 3145732
  57.0 22.3 %all-to-all-start.1 = ((bf16[32,64,128]{2,1,0:T(8,128)(2,1)}), bf16[32,64,128]{2,1,0:T(8,128)(2,1)S(1)}, u32[]{:S(2)}, u32[]{:S(2)}) async-start(bf16[32,64,128]{2,1,0:T(8,128)(2,1)} %ladder_terms.3.after_ref), calls=%async_computation.1 | async-start | bytes 1048576 | tf_op jit(solution)/shard_map/all_to_all | solution.py:377
  62.0 0.7 copy-start.2
  62.0 0.7 copy-start.3
  63.7 15.6 %copy-start.4 = (s32[16]{0:T(128)S(1)}, s32[16]{0:T(128)}, u32[]{:S(2)}) copy-start(s32[16]{0:T(128)} %get-tuple-element.7.slot_ref) | copy-start | bytes 196

commit v6 on v5

--- a/solution.py
+++ b/solution.py
@@ -58,7 +58,7 @@
                         out_ref[2 * v + half, 1, :, lanes] = woven[spot].astype(jnp.bfloat16)
         return carry
 
-    lax.fori_loop(0, factor_ref.shape[0], one, 0, unroll=4)
+    lax.fori_loop(0, factor_ref.shape[0], one, 0, unroll=8)
 
 
 def arrange_factors(factors):

time: 81.5 us -> 81.6 us (level)
  no operation moved by 1% of the time
where the time goes in v6:
time: 81.6 us; the launch traced here: 80.9 us
  starting transfers between devices  35.6 us (44%)
  waiting for transfers between devices  21.8 us (27%)
  Pallas kernels  18.7 us (23%)
  local copies, waits for them, and re-layouts  4.62 us (6%)
    all_to_all x1, waiting for transfers between devices, local(): lax.all_to_all(terms, 'tile', split_axis=0, concat_axis=0, tiled=True)  15.6 us
    all_to_all x1, starting transfers between devices, local(): lax.all_to_all(packed, 'tile', split_axis=0, concat_axis=0, tiled=True)  13.8 us
    pallas_call x2, Pallas kernels, ladder_terms(): pl.pallas_call(lambda *refs: ladder_kernel(places, more, *refs), out_shap...  12.9 us
    all_to_all x1, waiting for transfers between devices, local(): lax.all_to_all(packed, 'tile', split_axis=0, concat_axis=0, tiled=True)  6.16 us
    ppermute x1, starting transfers between devices, local(): far_first = lax.ppermute(below[:FAR_UP], 'rep', up)  5.45 us
    all_to_all x1, starting transfers between devices, local(): lax.all_to_all(terms, 'tile', split_axis=0, concat_axis=0, tiled=True)  4.98 us
    ppermute x1, starting transfers between devices, local(): far_second = lax.ppermute(above[FAR_UP:], 'rep', down)  4.27 us
    ppermute x1, starting transfers between devices, local(): below = lax.ppermute(own, 'rep', up)  3.95 us
  transfers between devices with their start and end apart: 6, of which 2 were waited for; matrix products, arithmetic and copies ran while one was open for 4% of the time, Pallas kernels for 15%

profile of v6, /device:TPU:1, one launch (start us, length us, event | category | flops | bytes accessed | tf_op | source)
XLA Modules:
  0.0 80.9 jit_solution(7815332511855730553)
XLA Ops:
  0.0 0.0 copy-start.1
  0.0 1.2 %copy-done.1 = bf16[8,2,8,4096]{3,2,1,0:T(8,128)(2,1)S(1)} copy-done((bf16[8,2,8,4096]{3,2,1,0:T(8,128)(2,1)S(1)}, bf16[8,2,8,4096]{3,2,1,0:T(8,128)(2,1)}, u32[]{:S(2)}) %copy-start.1) | copy-done | bytes 1048600
  1.2 0.9 %arrange_factors.1.refs_1_ = bf16[16,2,64,256]{3,2,1,0:T(8,128)(2,1)S(1)} custom-call(bf16[8,2,8,4096]{3,2,1,0:T(8,128)(2,1)S(1)} %copy-done.1), custom_call_target="tpu_custom_call" | custom-call | tf_op jit(solution)/shard_map/arrange_factors/pallas_call | solution.py:66
  2.1 3.9 %collective-permute-start = (bf16[16,2,64,256]{3,2,1,0:T(8,128)(2,1)S(1)}, bf16[16,2,64,256]{3,2,1,0:T(8,128)(2,1)S(1)}, u32[]{:S(2)}, u32[]{:S(2)}) collective-permute-start(bf16[16,2,64,256]{3,2,1,0:T(8,128)(2,1)S(1)} %arrange_factors.1.refs_1_), channel_id=1, source_target_pairs={{0,1},{1,2},{2,3},{3,0},{4,5},{5,6},{6,7},{7,4},{8,9},{9,10},{10,1... | collective-permute-start | bytes 3145736 | tf_op jit(solution)/shard_map/ppermute | solution.py:367
  6.1 3.2 %collective-permute-start.2 = (bf16[16,2,64,256]{3,2,1,0:T(8,128)(2,1)S(1)}, bf16[16,2,64,256]{3,2,1,0:T(8,128)(2,1)}, u32[]{:S(2)}, u32[]{:S(2)}) collective-permute-start(bf16[16,2,64,256]{3,2,1,0:T(8,128)(2,1)S(1)} %arrange_factors.1.refs_1_), channel_id=1, source_target_pairs={{0,3},{1,0},{2,1},{3,2},{4,7},{5,4},{6,5},{7,6},{8,11},{9,8},{10,9... | collective-permute-start | bytes 3145736 | tf_op jit(solution)/shard_map/ppermute | solution.py:368
  9.3 2.4 %pack_tiles.1 = (bf16[16,144,128]{2,1,0:T(8,128)(2,1)}, s32[16]{0:T(128)}) custom-call(s32[1]{0:T(128)} %bitcast.lead_ref, s32[2,16]{1,0:T(2,128)} %bitcast.2, s32[16]{0:T(128)} %live_hbm.3, s32[128]{0:T(128)} %owner_hbm.1, bf16[16,8,4096]{2,1,0:T(8,128)(2,1)} %amp_ref.1), custom_call_target="tpu_custom_call" | custom-call | tf_op jit(solution)/shard_map/pack_tiles/pallas_call | solution.py:138
  11.7 13.8 %all-to-all-start = ((bf16[16,144,128]{2,1,0:T(8,128)(2,1)}), bf16[16,144,128]{2,1,0:T(8,128)(2,1)S(1)}, u32[]{:S(2)}, u32[]{:S(2)}) async-start(bf16[16,144,128]{2,1,0:T(8,128)(2,1)} %get-tuple-element.8), calls=%async_computation | async-start | bytes 1179648 | tf_op jit(solution)/shard_map/all_to_all | solution.py:373
  25.5 0.0 collective-permute-done.refs_2_
  25.5 0.9 %slice.8 = bf16[9,2,64,256]{3,2,1,0:T(8,128)(2,1)} slice(bf16[16,2,64,256]{3,2,1,0:T(8,128)(2,1)S(1)} %collective-permute-done.refs_2_), slice={[0:9], [0:2], [0:64], [0:256]} | slice | bytes 1179648 | tf_op jit(solution)/shard_map/slice | solution.py:369
  26.4 5.4 %collective-permute-start.1 = (bf16[9,2,64,256]{3,2,1,0:T(8,128)(2,1)}, bf16[9,2,64,256]{3,2,1,0:T(8,128)(2,1)S(1)}, u32[]{:S(2)}, u32[]{:S(2)}) collective-permute-start(bf16[9,2,64,256]{3,2,1,0:T(8,128)(2,1)} %slice.8), channel_id=1, source_target_pairs={{0,1},{1,2},{2,3},{3,0},{4,5},{5,6},{6,7},{7,4},{8,9},{9,10},{10,1... | collective-permute-start | bytes 1769480 | tf_op jit(solution)/shard_map/ppermute | solution.py:369
  31.9 0.0 collective-permute-done.2.refs_3_
  31.9 1.8 %slice.9 = bf16[7,2,64,256]{3,2,1,0:T(8,128)(2,1)} slice(bf16[16,2,64,256]{3,2,1,0:T(8,128)(2,1)} %collective-permute-done.2.refs_3_), slice={[9:16], [0:2], [0:64], [0:256]} | slice | bytes 917504 | tf_op jit(solution)/shard_map/slice | solution.py:370
  33.7 4.3 %collective-permute-start.3 = (bf16[7,2,64,256]{3,2,1,0:T(8,128)(2,1)}, bf16[7,2,64,256]{3,2,1,0:T(8,128)(2,1)}, u32[]{:S(2)}, u32[]{:S(2)}) collective-permute-start(bf16[7,2,64,256]{3,2,1,0:T(8,128)(2,1)} %slice.9), channel_id=1, source_target_pairs={{0,3},{1,0},{2,1},{3,2},{4,7},{5,4},{6,5},{7,6},{8,11},{9,8},{10,9... | collective-permute-start | bytes 1376264 | tf_op jit(solution)/shard_map/ppermute | solution.py:370
  38.0 6.2 %all-to-all-done.refs_0_ = bf16[16,144,128]{2,1,0:T(8,128)(2,1)S(1)} async-done(((bf16[16,144,128]{2,1,0:T(8,128)(2,1)}), bf16[16,144,128]{2,1,0:T(8,128)(2,1)S(1)}, u32[]{:S(2)}, u32[]{:S(2)}) %all-to-all-start) | async-done | bytes 589856 | tf_op jit(solution)/shard_map/all_to_all | solution.py:373
  44.2 8.4 %ladder_terms.2.refs_3_ = f32[32,64,128]{2,1,0:T(8,128)S(1)} custom-call(bf16[16,144,128]{2,1,0:T(8,128)(2,1)S(1)} %all-to-all-done.refs_0_, bf16[16,2,64,256]{3,2,1,0:T(8,128)(2,1)S(1)} %arrange_factors.1.refs_1_, bf16[16,2,64,256]{3,2,1,0:T(8,128)(2,1)S(1)} %collective-permute-done.refs_2_, bf16[16,2,64,256]{3,2,1,0:T(8,128)(2,1)} %collective-permute-done.2.refs_3_), custom_call_target="tpu_custom_call" | custom-call | flops 10000000 | bytes 3145728 | tf_op jit(solution)/shard_map/ladder_terms/pallas_call | solution.py:268
  52.6 0.0 collective-permute-done.3.refs_2_
  52.6 0.0 collective-permute-done.1.refs_1_
  52.6 0.0 copy-start.5
  52.6 4.5 %ladder_terms.3.after_ref = bf16[32,64,128]{2,1,0:T(8,128)(2,1)} custom-call(bf16[16,144,128]{2,1,0:T(8,128)(2,1)S(1)} %all-to-all-done.refs_0_, bf16[9,2,64,256]{3,2,1,0:T(8,128)(2,1)S(1)} %collective-permute-done.1.refs_1_, bf16[7,2,64,256]{3,2,1,0:T(8,128)(2,1)} %collective-permute-done.3.refs_2_, f32[32,64,128]{2,1,0:T(8,128)S(1)} %ladder_terms.2.refs_3_), custom_call_target="tpu_custom_call" | custom-call | flops 10000000 | bytes 1048576 | tf_op jit(solution)/shard_map/ladder_terms/pallas_call | solution.py:268
  57.1 0.0 copy-start
  57.1 5.0 %all-to-all-start.1 = ((bf16[32,64,128]{2,1,0:T(8,128)(2,1)}), bf16[32,64,128]{2,1,0:T(8,128)(2,1)S(1)}, u32[]{:S(2)}, u32[]{:S(2)}) async-start(bf16[32,64,128]{2,1,0:T(8,128)(2,1)} %ladder_terms.3.after_ref), calls=%async_computation.1 | async-start | bytes 1048576 | tf_op jit(solution)/shard_map/all_to_all | solution.py:377
  62.1 0.0 copy-done.5
  62.1 0.0 copy-start.2
  62.1 0.0 copy-start.3
  62.1 0.1 copy.7.coupling_ref
  62.2 0.0 copy-done
  62.2 0.5 copy-done.2
  62.8 0.0 copy-done.3
  62.8 1.0 %cycle_terms.1.cycle_ref = f32[32,4096]{1,0:T(8,128)S(1)} custom-call(s32[1]{0:T(128)} %bitcast.lead_ref, s32[2,16]{1,0:T(2,128)S(1)} %bitcast.3, s32[16]{0:T(128)S(1)} %copy-done.3, bf16[64,8,8]{2,1,0:T(8,128)(2,1)S(1)} %copy.7.coupling_ref, bf16[16,8,4096]{2,1,0:T(8,128)(2,1)S(1)} %copy-done, bf16[32,64,128]{2,1,0:T(8,128)(2,1)} %ladder_terms.3.after_ref), custom_call_target="tpu_custom_call" | custom-call | tf_op jit(solution)/shard_map/cycle_terms/pallas_call | solution.py:340
  63.8 0.0 copy-start.4
  63.8 15.6 %all-to-all-done.1.returned_ref = bf16[32,64,128]{2,1,0:T(8,128)(2,1)S(1)} async-done(((bf16[32,64,128]{2,1,0:T(8,128)(2,1)}), bf16[32,64,128]{2,1,0:T(8,128)(2,1)S(1)}, u32[]{:S(2)}, u32[]{:S(2)}) %all-to-all-start.1) | async-done | bytes 524320 | tf_op jit(solution)/shard_map/all_to_all | solution.py:377
  79.4 0.0 copy-done.4
  79.4 1.5 %finish_tiles.1 = bf16[16,2,4096]{2,1,0:T(2,128)(2,1)} custom-call(s32[16]{0:T(128)S(1)} %copy-done.4, bf16[32,64,128]{2,1,0:T(8,128)(2,1)S(1)} %all-to-all-done.1.returned_ref, f32[32,4096]{1,0:T(8,128)S(1)} %cycle_terms.1.cycle_ref), custom_call_target="tpu_custom_call" | custom-call | tf_op jit(solution)/shard_map/finish_tiles/pallas_call | solution.py:296
Async XLA Ops:
  0.0 1.2 %copy-start.1 = (bf16[8,2,8,4096]{3,2,1,0:T(8,128)(2,1)S(1)}, bf16[8,2,8,4096]{3,2,1,0:T(8,128)(2,1)}, u32[]{:S(2)}) copy-start(bf16[8,2,8,4096]{3,2,1,0:T(8,128)(2,1)} %factor_ref.1) | copy-start | bytes 3145732
  2.1 23.4 %collective-permute-start = (bf16[16,2,64,256]{3,2,1,0:T(8,128)(2,1)S(1)}, bf16[16,2,64,256]{3,2,1,0:T(8,128)(2,1)S(1)}, u32[]{:S(2)}, u32[]{:S(2)}) collective-permute-start(bf16[16,2,64,256]{3,2,1,0:T(8,128)(2,1)S(1)} %arrange_factors.1.refs_1_), channel_id=1, source_target_pairs={{0,1},{1,2},{2,3},{3,0},{4,5},{5,6},{6,7},{7,4},{8,9},{9,10},{10,1... | collective-permute-start | bytes 3145736 | tf_op jit(solution)/shard_map/ppermute | solution.py:367
  6.1 25.8 %collective-permute-start.2 = (bf16[16,2,64,256]{3,2,1,0:T(8,128)(2,1)S(1)}, bf16[16,2,64,256]{3,2,1,0:T(8,128)(2,1)}, u32[]{:S(2)}, u32[]{:S(2)}) collective-permute-start(bf16[16,2,64,256]{3,2,1,0:T(8,128)(2,1)S(1)} %arrange_factors.1.refs_1_), channel_id=1, source_target_pairs={{0,3},{1,0},{2,1},{3,2},{4,7},{5,4},{6,5},{7,6},{8,11},{9,8},{10,9... | collective-permute-start | bytes 3145736 | tf_op jit(solution)/shard_map/ppermute | solution.py:368
  11.7 32.5 %all-to-all-start = ((bf16[16,144,128]{2,1,0:T(8,128)(2,1)}), bf16[16,144,128]{2,1,0:T(8,128)(2,1)S(1)}, u32[]{:S(2)}, u32[]{:S(2)}) async-start(bf16[16,144,128]{2,1,0:T(8,128)(2,1)} %get-tuple-element.8), calls=%async_computation | async-start | bytes 1179648 | tf_op jit(solution)/shard_map/all_to_all | solution.py:373
  26.4 26.2 %collective-permute-start.1 = (bf16[9,2,64,256]{3,2,1,0:T(8,128)(2,1)}, bf16[9,2,64,256]{3,2,1,0:T(8,128)(2,1)S(1)}, u32[]{:S(2)}, u32[]{:S(2)}) collective-permute-start(bf16[9,2,64,256]{3,2,1,0:T(8,128)(2,1)} %slice.8), channel_id=1, source_target_pairs={{0,1},{1,2},{2,3},{3,0},{4,5},{5,6},{6,7},{7,4},{8,9},{9,10},{10,1... | collective-permute-start | bytes 1769480 | tf_op jit(solution)/shard_map/ppermute | solution.py:369
  33.7 18.8 %collective-permute-start.3 = (bf16[7,2,64,256]{3,2,1,0:T(8,128)(2,1)}, bf16[7,2,64,256]{3,2,1,0:T(8,128)(2,1)}, u32[]{:S(2)}, u32[]{:S(2)}) collective-permute-start(bf16[7,2,64,256]{3,2,1,0:T(8,128)(2,1)} %slice.9), channel_id=1, source_target_pairs={{0,3},{1,0},{2,1},{3,2},{4,7},{5,4},{6,5},{7,6},{8,11},{9,8},{10,9... | collective-permute-start | bytes 1376264 | tf_op jit(solution)/shard_map/ppermute | solution.py:370
  52.6 9.5 %copy-start.5 = (bf16[64,8,8]{0,2,1:T(8,128)(2,1)S(1)}, bf16[64,8,8]{0,2,1:T(8,128)(2,1)}, u32[]{:S(2)}) copy-start(bf16[64,8,8]{0,2,1:T(8,128)(2,1)} %param.10) | copy-start | bytes 24580
  57.1 5.2 %copy-start = (bf16[16,8,4096]{2,1,0:T(8,128)(2,1)S(1)}, bf16[16,8,4096]{2,1,0:T(8,128)(2,1)}, u32[]{:S(2)}) copy-start(bf16[16,8,4096]{2,1,0:T(8,128)(2,1)} %amp_ref.1) | copy-start | bytes 3145732
  57.1 22.3 %all-to-all-start.1 = ((bf16[32,64,128]{2,1,0:T(8,128)(2,1)}), bf16[32,64,128]{2,1,0:T(8,128)(2,1)S(1)}, u32[]{:S(2)}, u32[]{:S(2)}) async-start(bf16[32,64,128]{2,1,0:T(8,128)(2,1)} %ladder_terms.3.after_ref), calls=%async_computation.1 | async-start | bytes 1048576 | tf_op jit(solution)/shard_map/all_to_all | solution.py:377
  62.1 0.7 copy-start.2
  62.1 0.7 copy-start.3
  63.8 15.6 %copy-start.4 = (s32[16]{0:T(128)S(1)}, s32[16]{0:T(128)}, u32[]{:S(2)}) copy-start(s32[16]{0:T(128)} %get-tuple-element.7.slot_ref) | copy-start | bytes 196
